TPU v7x, 32 devices: a whole 2x2x4 slice. The times are simulated.
32 devices in a mesh: section: 4 (over y, core), fsdp: 4 (over z), tp: 2 (over x).
Axes of the slice: x: 2, y: 2, z: 4, core: 2. Of those that a mesh axis runs over, the one named last changes fastest.
Arguments:
- text_tokens: bfloat16 [4096, 8192], P(('section', 'fsdp')), may hold values from -45 to 45
- images: bfloat16 [16, 256, 8192], P('section', None, ('fsdp', 'tp')), may hold values from -45 to 45
- counts: int32 [16], P('section'), may hold values from 1 to 256, as said below
- offsets: int32 [16], P('section'), may hold values from 0 to 4095, as said below
- norm_gain: float32 [8192], replicated, may hold values from 0.25 to 1.75
- value_weight: bfloat16 [8192, 512], P(('fsdp', 'tp'), 'section'), may hold values from -0.0625 to 0.0625
- value_grad: bfloat16 [4096, 512], P(('section', 'fsdp')), may hold values from -6 to 6
Outputs:
- values: bfloat16 [4096, 512], P(('section', 'fsdp'), 'tp')
- visual_grads: bfloat16 [16, 256, 8192], P('section', None, ('fsdp', 'tp'))
Inputs may be any that keep to these rules, and one draw needn't show every extreme that they name: `counts`: on every section index some tile has exactly 256 visual tokens. Tile i occupies positions offsets[i] to offsets[i] + counts[i] - 1, all inside one aligned block of 256 positions. The positions of one section index form 4 such blocks. The 4 tiles of one section index go to 4 different section indices, and every block receives exactly one tile.
All inputs are finite; a program needn't handle non-finite values.
Results may differ from a plain program's by a relative error of at most 0.0049.
Values may be sent and summed in bfloat16 or wider, within the bound.
A program may use at most 64 MiB of HBM per device.

v0:
```python
import jax
import jax.numpy as jnp
from jax import lax
from jax.sharding import PartitionSpec as P

epsilon = 1e-05


def on_device(text_tokens, images, counts, offsets, norm_gain, value_weight, value_grad):
    sections = lax.axis_size("section")
    columns = lax.axis_size("fsdp")
    pair_count = lax.axis_size("tp")
    tok_rows, feature_width = text_tokens.shape
    img_count, most_slots, feature_slice = images.shape
    group_rows = columns * tok_rows
    pair_index = lax.axis_index("tp")
    column_index = lax.axis_index("fsdp")
    target = offsets // group_rows
    within = offsets % group_rows
    region = within // most_slots
    first_slot = within % most_slots
    section_ids = jnp.arange(sections, dtype=jnp.int32)
    slot_ids = jnp.arange(most_slots, dtype=jnp.int32)
    is_valid = slot_ids[None, :] < counts[:, None]
    placing = (
        (slot_ids[None, :, None] == first_slot[:, None, None] + slot_ids[None, None, :])
        & is_valid[:, None, :]
    ).astype(jnp.bfloat16)
    routing = target[:, None] == section_ids[None, :]
    route_float = routing.astype(jnp.bfloat16)
    route_int = routing.astype(jnp.int32)
    meta_rows = jnp.stack([region, first_slot, counts], axis=1)
    meta_out = jnp.sum(route_int[:, :, None] * meta_rows[:, None, :], axis=0)
    w_rows = lax.all_gather(value_weight, "fsdp", axis=0, tiled=True)
    w_own = lax.all_gather(w_rows, "section", axis=1, tiled=True)
    placed = jnp.einsum("krj,kjd->krd", placing, images, preferred_element_type=jnp.float32).astype(
        jnp.bfloat16
    )
    outgoing = jnp.einsum(
        "kt,krd->trd", route_float, placed, preferred_element_type=jnp.float32
    ).astype(jnp.bfloat16)
    arrived, meta_in = (
        lax.all_to_all(outgoing, "section", split_axis=0, concat_axis=0, tiled=True),
        lax.all_to_all(meta_out, "section", split_axis=0, concat_axis=0, tiled=True),
    )
    order_int = (meta_in[:, 0:1] == section_ids[None, :]).astype(jnp.int32)
    order_float = order_int.astype(jnp.bfloat16)
    by_region = jnp.einsum(
        "sr,spd->rpd", order_float, arrived, preferred_element_type=jnp.float32
    ).astype(jnp.bfloat16)
    rows_in = lax.all_to_all(
        by_region.reshape(sections * most_slots, feature_slice),
        "fsdp",
        split_axis=0,
        concat_axis=1,
        tiled=True,
    )
    region_start = jnp.sum(order_int * meta_in[:, 1:2], axis=0)
    region_count = jnp.sum(order_int * meta_in[:, 2:3], axis=0)
    row_ids = column_index * tok_rows + jnp.arange(tok_rows, dtype=jnp.int32)
    row_region = ((row_ids // most_slots)[:, None] == section_ids[None, :]).astype(jnp.int32)
    row_local = row_ids % most_slots
    row_start = jnp.sum(row_region * region_start[None, :], axis=1)
    row_count = jnp.sum(row_region * region_count[None, :], axis=1)
    covered = (row_local >= row_start) & (row_local < row_start + row_count)
    text_own = lax.dynamic_index_in_dim(
        text_tokens.reshape(tok_rows, columns, pair_count, feature_slice),
        pair_index,
        2,
        keepdims=False,
    ).reshape(tok_rows, columns * feature_slice)
    gain_own = lax.dynamic_index_in_dim(
        norm_gain.reshape(columns, pair_count, feature_slice), pair_index, 1, keepdims=False
    ).reshape(-1)
    mixed_rows = jnp.where(covered[:, None], rows_in, text_own)
    mixed_f = mixed_rows.astype(jnp.float32)
    grad_normed = lax.dot_general(
        value_grad, w_own, (((1,), (1,)), ((), ())), preferred_element_type=jnp.float32
    )
    weighted = grad_normed * gain_own
    square_sum, inner_sum = lax.psum(
        (jnp.sum(mixed_f * mixed_f, axis=1), jnp.sum(weighted * mixed_f, axis=1)), "tp"
    )
    inv_rms = lax.rsqrt(square_sum / feature_width + epsilon)[:, None]
    normed = (mixed_f * inv_rms * gain_own).astype(jnp.bfloat16)
    head_part = jnp.dot(normed, w_own, preferred_element_type=jnp.float32)
    values = lax.psum_scatter(head_part, "tp", scatter_dimension=1, tiled=True).astype(jnp.bfloat16)
    grad_own = (
        inv_rms * weighted
        - mixed_f * (inv_rms * inv_rms * inv_rms) * inner_sum[:, None] / feature_width
    ).astype(jnp.bfloat16)
    back_rows = lax.all_to_all(grad_own, "fsdp", split_axis=1, concat_axis=0, tiled=True)
    by_source = jnp.einsum(
        "sr,rpd->spd",
        order_float,
        back_rows.reshape(sections, most_slots, feature_slice),
        preferred_element_type=jnp.float32,
    ).astype(jnp.bfloat16)
    returned = lax.all_to_all(by_source, "section", split_axis=0, concat_axis=0, tiled=True)
    own_rows = jnp.einsum(
        "kt,trd->krd", route_float, returned, preferred_element_type=jnp.float32
    ).astype(jnp.bfloat16)
    visual_grads = jnp.einsum(
        "krj,krd->kjd", placing, own_rows, preferred_element_type=jnp.float32
    ).astype(jnp.bfloat16)
    return (values, visual_grads)


def solution(mesh):
    placed = (
        P(("section", "fsdp"), None),
        P("section", None, ("fsdp", "tp")),
        P("section"),
        P("section"),
        P(),
        P(("fsdp", "tp"), "section"),
        P(("section", "fsdp"), None),
    )
    return jax.shard_map(
        on_device,
        mesh=mesh,
        in_specs=placed,
        out_specs=(P(("section", "fsdp"), "tp"), P("section", None, ("fsdp", "tp"))),
        check_vma=False,
    )
```

profile of v0, /device:TPU:0, one launch (start us, length us, event | category | flops | bytes accessed | tf_op | source)
XLA Modules:
  0.0 275.7 jit_solution(15366117122934841921)
XLA Ops:
  7.2 0.0 copy-start
  7.2 0.0 all-gather.3.cloned.1.call-start
  7.2 0.7 all-gather.3.cloned.1.call-update
  7.9 0.7 fusion.57
  8.6 0.7 and_select_fusion
  9.3 0.7 pad_add_fusion
  9.9 0.1 fusion.46
  10.0 0.1 multiply_reduce_fusion.1
  10.1 0.7 copy.46
  10.7 4.2 %all-to-all-start = ((s32[4,1,3]{2,1,0:T(1,128)}), s32[4,1,3]{2,1,0:T(1,128)S(1)}, u32[]{:S(2)}, u32[]{:S(2)}) async-start(s32[4,1,3]{2,1,0:T(1,128)} %copy.46), calls=%async_computation | async-start | bytes 4096 | tf_op jit(solution)/shard_map/all_to_all | solution.py:44
  15.0 0.1 iota_add_fusion
  15.1 25.2 %all-gather.3.cloned.1.call-done = bf16[4096,128]{1,0:T(8,128)(2,1)} async-done(((bf16[1024,128]{1,0:T(8,128)(2,1)}), bf16[4096,128]{1,0:T(8,128)(2,1)}) %all-gather.3.cloned.1.call-update) | async-done | bytes 1048592 | tf_op jit(solution)/shard_map/all_gather | solution.py:34
  40.2 0.0 all-gather.5.cloned.1.call-update
  40.3 0.7 iota_compare_fusion.1
  41.0 1.4 convolution_convert_fusion
  42.4 2.2 fusion.29
  44.6 1.9 copy.50
  46.6 4.5 %all-to-all-start.1 = ((bf16[4,256,1024]{2,1,0:T(8,128)(2,1)}), bf16[4,256,1024]{2,1,0:T(8,128)(2,1)}, u32[]{:S(2)}, u32[]{:S(2)}) async-start(bf16[4,256,1024]{2,1,0:T(8,128)(2,1)} %copy.50), calls=%async_computation.1 | async-start | bytes 4194304 | tf_op jit(solution)/shard_map/all_to_all | solution.py:43
  51.1 0.2 slice_reduce_fusion
  51.3 45.5 %all-to-all-done.1 = bf16[4,256,1024]{2,1,0:T(8,128)(2,1)} async-done(((bf16[4,256,1024]{2,1,0:T(8,128)(2,1)}), bf16[4,256,1024]{2,1,0:T(8,128)(2,1)}, u32[]{:S(2)}, u32[]{:S(2)}) %all-to-all-start.1) | async-done | bytes 2097184 | tf_op jit(solution)/shard_map/all_to_all | solution.py:43
  96.8 4.0 %fusion.23 = bf16[4,256,1024]{2,0,1:T(4,128)(2,1)S(1)} fusion(bf16[4,256,1024]{2,1,0:T(8,128)(2,1)} %all-to-all-done.1, s32[4]{0:T(128)S(1)} %get-tuple-element.4), kind=kOutput, calls=%fused_computation.30 | convolution fusion | flops 9437232 | bytes 4194320 | tf_op jit(solution)/shard_map/sr,spd->rpd/dot_general | solution.py:48
  100.7 1.9 copy.53
  102.7 4.8 %all-to-all-start.2 = ((bf16[4,256,1024]{2,1,0:T(8,128)(2,1)}), bf16[4,256,1024]{2,1,0:T(8,128)(2,1)}, u32[]{:S(2)}, u32[]{:S(2)}) async-start(bf16[4,256,1024]{2,1,0:T(8,128)(2,1)} %copy.53), calls=%async_computation.2 | async-start | bytes 4194304 | tf_op jit(solution)/shard_map/all_to_all | solution.py:51
  107.5 7.9 %reshape.144 = bf16[256,4,2,1024]{3,2,1,0:T(2,128)(2,1)} reshape(bf16[256,8192]{1,0:T(8,128)(2,1)} %param.7) | data formatting | bytes 8388608 | tf_op jit(solution)/shard_map/reshape | solution.py:67
  115.4 16.6 %fusion.58 = (bf16[256,4,1024]{2,1,0:T(4,128)(2,1)S(1)}, bf16[256,4,1,1024]{3,2,1,0:T(2,128)(2,1)}) fusion(bf16[256,4,2,1024]{3,2,1,0:T(2,128)(2,1)} %reshape.144, s32[]{:T(128)S(6)} %select_n.57), kind=kLoop, calls=%fused_computation.88 | loop fusion | bytes 6291460 | tf_op jit(solution)/shard_map/jit(dynamic_index_in_dim)/dynamic_slice | solution.py:66
  132.0 2.2 copy.73
  134.3 0.1 select_reduce_fusion.2
  134.4 0.1 select_reduce_fusion
  134.5 21.4 %all-to-all-done.2 = bf16[4,256,1024]{2,1,0:T(8,128)(2,1)} async-done(((bf16[4,256,1024]{2,1,0:T(8,128)(2,1)}), bf16[4,256,1024]{2,1,0:T(8,128)(2,1)}, u32[]{:S(2)}, u32[]{:S(2)}) %all-to-all-start.2) | async-done | bytes 2097184 | tf_op jit(solution)/shard_map/all_to_all | solution.py:51
  155.9 3.3 %copy.72 = bf16[4,32,8,1024]{3,2,0,1:T(8,128)(2,1)} copy(bf16[4,32,8,1024]{3,2,1,0:T(8,128)(2,1)} %bitcast.15) | data formatting | bytes 4194304 | tf_op jit(solution)/shard_map/all_to_all | solution.py:51
  159.2 4.0 %multiply_reduce_fusion = f32[256]{0:T(256)S(1)} fusion(bf16[256,4,1,1024]{3,2,1,0:T(2,128)(2,1)S(1)} %copy-done.1, bf16[4,256,1024]{2,1,0:T(8,128)(2,1)} %all-to-all-done.2, pred[256]{0:T(512)(128)(4,1)S(1)} %compare_and_fusion), kind=kLoop, calls=%fused_computation.11 | loop fusion | flops 4194048 | bytes 4195584 | tf_op jit(solution)/shard_map/reduce_sum | solution.py:82
  163.3 0.0 all-gather.5.cloned.1.call-done
  163.3 7.4 %fusion.6 = (f32[256]{0:T(256)S(1)}, bf16[256,4096]{1,0:T(8,128)(2,1)}, f32[256,4096]{1,0:T(8,128)}) fusion(bf16[256,4096]{1,0:T(8,128)(2,1)} %bitcast.45, bf16[256,4096]{1,0:T(8,128)(2,1)} %bitcast.44, pred[256]{0:T(512)(128)(4,1)S(1)} %compare_and_fusion, f32[4096]{0:T(1024)S(1)} %bitcast.47, bf16[256,512]{1,0:T(8,128)(2,1)S(1)} %copy-done.2, ...), kind=kOutput, calls=%fused_computation.10 | convolution fusion | flops 1078984448 | bytes 14959872 | tf_op jit(solution)/shard_map/dot_general | solution.py:77
  170.7 4.9 %all-reduce = (f32[256]{0:T(256)S(1)}, f32[256]{0:T(256)S(1)}) all-reduce(f32[256]{0:T(256)S(1)} %multiply_reduce_fusion, f32[256]{0:T(256)S(1)} %get-tuple-element.11), channel_id=1, replica_groups=mesh['section'=4,'fsdp'=4,'tp'=2] {'tp'}, use_global_device_ids=true, to_apply=%region_6.7 | all-reduce | flops 512 | bytes 4096 | tf_op jit(solution)/shard_map/psum | solution.py:81
  175.6 4.1 %fusion.5 = bf16[256,4096]{1,0:T(8,128)(2,1)S(1)} fusion(bf16[256,4096]{1,0:T(8,128)(2,1)} %get-tuple-element.12, f32[256,4096]{1,0:T(8,128)} %get-tuple-element.20, f32[256]{0:T(256)S(1)} %get-tuple-element.10, f32[256]{0:T(256)S(1)} %get-tuple-element.18, f32[256]{0:T(256)S(1)} %get-tuple-element.19), kind=kLoop, calls=%fused_computation.9 | loop fusion | flops 7340032 | bytes 8391680 | tf_op jit(solution)/shard_map/convert_element_type | solution.py:91
  179.7 0.2 copy.102
  179.9 49.0 %all_to_all.54 = bf16[256,4,1024]{2,0,1:T(8,128)(2,1)S(1)} all-to-all(bf16[256,4,1024]{2,0,1:T(8,128)(2,1)S(1)} %bitcast.43), channel_id=1, replica_groups=mesh['section'=4,'fsdp'=4,'tp'=2] {'fsdp'}, dimensions={1} | all-to-all | bytes 4194304 | tf_op jit(solution)/shard_map/all_to_all | solution.py:92
  229.0 1.8 fusion.26
  230.7 2.0 copy.59
  232.7 4.4 %all-to-all-start.4 = ((bf16[4,256,1024]{2,1,0:T(8,128)(2,1)}), bf16[4,256,1024]{2,1,0:T(8,128)(2,1)}, u32[]{:S(2)}, u32[]{:S(2)}) async-start(bf16[4,256,1024]{2,1,0:T(8,128)(2,1)} %copy.59), calls=%async_computation.5 | async-start | bytes 4194304 | tf_op jit(solution)/shard_map/all_to_all | solution.py:99
  237.2 0.0 reduce-scatter.2.cloned.1.call-start
  237.2 5.0 %fusion.7 = f32[256,512]{1,0:T(8,128)} fusion(bf16[4096,512]{1,0:T(8,128)(2,1)} %all-gather.5.cloned.1.call-done, bf16[256,4096]{1,0:T(8,128)(2,1)} %get-tuple-element.12, f32[4096]{0:T(1024)S(1)} %bitcast.48, f32[256]{0:T(256)S(1)} %get-tuple-element.19), kind=kOutput, calls=%fused_computation.12 | convolution fusion | flops 1077936128 | bytes 6833152 | tf_op jit(solution)/shard_map/dot_general | solution.py:86
  242.2 0.0 reduce-scatter.2.cloned.1.call-update
  242.2 14.2 %reduce-scatter.2.cloned.1.call-done = f32[256,256]{1,0:T(8,128)} async-done(((f32[256,512]{1,0:T(8,128)}), f32[256,256]{1,0:T(8,128)}) %reduce-scatter.2.cloned.1.call-update) | async-done | bytes 262160 | tf_op jit(solution)/shard_map/reduce_scatter | solution.py:87
  256.4 1.6 convert_element_type.58
  258.0 4.9 %all-to-all-done.4 = bf16[4,256,1024]{2,1,0:T(8,128)(2,1)} async-done(((bf16[4,256,1024]{2,1,0:T(8,128)(2,1)}), bf16[4,256,1024]{2,1,0:T(8,128)(2,1)}, u32[]{:S(2)}, u32[]{:S(2)}) %all-to-all-start.4) | async-done | bytes 2097184 | tf_op jit(solution)/shard_map/all_to_all | solution.py:99
  262.9 3.4 %fusion.32 = bf16[4,256,1024]{2,0,1:T(4,128)(2,1)S(1)} fusion(bf16[4,256,1024]{2,1,0:T(8,128)(2,1)} %all-to-all-done.4, s32[4]{0:T(128)S(1)} %get-tuple-element.22), kind=kOutput, calls=%fused_computation.33 | convolution fusion | flops 9437200 | bytes 4194320 | tf_op jit(solution)/shard_map/kt,trd->krd/dot_general | solution.py:100
  266.3 2.9 %fusion.35 = bf16[4,256,1024]{2,1,0:T(8,128)(2,1)} fusion(bf16[4,256,1024]{2,0,1:T(4,128)(2,1)S(1)} %fusion.32, s32[4,256]{1,0:T(4,128)S(1)} %iota_add_fusion, pred[4,256]{1,0:T(4,128)(4,1)S(1)} %iota_compare_fusion.1), kind=kOutput, calls=%fused_computation.34 | convolution fusion | flops 538443776 | bytes 4199424 | tf_op jit(solution)/shard_map/krj,krd->kjd/dot_general | solution.py:103
  (14 shorter events, 0.1 us)
Async XLA Ops:
  7.2 33.8 %copy-start = (bf16[4,256,1024]{2,1,0:T(8,128)(2,1)S(1)}, bf16[4,256,1024]{2,1,0:T(8,128)(2,1)}, u32[]{:S(2)}) copy-start(bf16[4,256,1024]{2,1,0:T(8,128)(2,1)} %param.8) | copy-start | bytes 6291460
  7.2 33.1 %all-gather.3.cloned.1.call-start = ((), (), s32[]{:S(2)}) async-start(), calls=%async_computation.6 | async-start | bytes 1310720 | tf_op jit(solution)/shard_map/all_gather | solution.py:34
  10.7 35.8 %all-to-all-start = ((s32[4,1,3]{2,1,0:T(1,128)}), s32[4,1,3]{2,1,0:T(1,128)S(1)}, u32[]{:S(2)}, u32[]{:S(2)}) async-start(s32[4,1,3]{2,1,0:T(1,128)} %copy.46), calls=%async_computation | async-start | bytes 4096 | tf_op jit(solution)/shard_map/all_to_all | solution.py:44
  15.0 148.3 %all-gather.5.cloned.1.call-start = ((), (), s32[]{:S(2)}) async-start(), calls=%async_computation.7 | async-start | bytes 5242880 | tf_op jit(solution)/shard_map/all_gather | solution.py:35
  46.6 50.2 %all-to-all-start.1 = ((bf16[4,256,1024]{2,1,0:T(8,128)(2,1)}), bf16[4,256,1024]{2,1,0:T(8,128)(2,1)}, u32[]{:S(2)}, u32[]{:S(2)}) async-start(bf16[4,256,1024]{2,1,0:T(8,128)(2,1)} %copy.50), calls=%async_computation.1 | async-start | bytes 4194304 | tf_op jit(solution)/shard_map/all_to_all | solution.py:43
  102.7 4.8 %copy-start.3 = (f32[8192]{0:T(1024)S(1)}, f32[8192]{0:T(1024)}, u32[]{:S(2)}) copy-start(f32[8192]{0:T(1024)} %param.11) | copy-start | bytes 98308
  102.7 53.3 %all-to-all-start.2 = ((bf16[4,256,1024]{2,1,0:T(8,128)(2,1)}), bf16[4,256,1024]{2,1,0:T(8,128)(2,1)}, u32[]{:S(2)}, u32[]{:S(2)}) async-start(bf16[4,256,1024]{2,1,0:T(8,128)(2,1)} %copy.53), calls=%async_computation.2 | async-start | bytes 4194304 | tf_op jit(solution)/shard_map/all_to_all | solution.py:51
  155.9 3.3 %copy-start.1 = (bf16[256,4,1,1024]{3,2,1,0:T(2,128)(2,1)S(1)}, bf16[256,4,1,1024]{3,2,1,0:T(2,128)(2,1)}, u32[]{:S(2)}) copy-start(bf16[256,4,1,1024]{3,2,1,0:T(2,128)(2,1)} %get-tuple-element.14) | copy-start | bytes 6291460
  159.2 4.1 %copy-start.2 = (bf16[256,512]{1,0:T(8,128)(2,1)S(1)}, bf16[256,512]{1,0:T(8,128)(2,1)}, u32[]{:S(2)}) copy-start(bf16[256,512]{1,0:T(8,128)(2,1)} %param.13) | copy-start | bytes 786436
  232.7 30.2 %all-to-all-start.4 = ((bf16[4,256,1024]{2,1,0:T(8,128)(2,1)}), bf16[4,256,1024]{2,1,0:T(8,128)(2,1)}, u32[]{:S(2)}, u32[]{:S(2)}) async-start(bf16[4,256,1024]{2,1,0:T(8,128)(2,1)} %copy.59), calls=%async_computation.5 | async-start | bytes 4194304 | tf_op jit(solution)/shard_map/all_to_all | solution.py:99
  237.2 19.2 %reduce-scatter.2.cloned.1.call-start = ((), (), s32[]{:S(2)}) async-start(), calls=%async_computation.8 | async-start | bytes 786432 | tf_op jit(solution)/shard_map/reduce_scatter | solution.py:87
Sparse Core Ops, SparseCore 0:
  9.6 30.6 all-gather.2
  41.8 54.5 all-gather.4
  242.3 14.0 reduce-scatter.1
where the time goes:
time: 277 us; the launch traced here: 276 us
  waiting for transfers between devices  112 us (40%)
  blocking collectives  54 us (19%)
  local copies, waits for them, and re-layouts  37 us (13%)
  matrix products  27.9 us (10%)
  starting transfers between devices  18 us (6%)
  between operations  13.9 us (5%)
  other arithmetic  12.9 us (5%)
    all_to_all x1, blocking collectives, on_device(): lax.all_to_all(grad_own, 'fsdp', split_axis=1, concat_axis=0, tiled=True)  49 us
    all_to_all x1, waiting for transfers between devices, on_device(): lax.all_to_all(outgoing, 'section', split_axis=0, concat_axis=0, tiled=True)  45.5 us
    all_gather x1, waiting for transfers between devices, on_device(): w_rows = lax.all_gather(value_weight, 'fsdp', axis=0, tiled=True)  25.2 us
    all_to_all x1, waiting for transfers between devices, on_device(): lax.all_to_all(by_region.reshape(sections * most_slots, feature_slice), '...  21.4 us
    dynamic_slice x1, local copies, waits for them, and re-layouts, on_device(): lax.dynamic_index_in_dim(text_tokens.reshape(tok_rows, columns, pair_coun...  16.6 us
    reduce_scatter x1, waiting for transfers between devices, on_device(): lax.psum_scatter(head_part, 'tp', scatter_dimension=1, tiled=True)  14.2 us
    reshape x1, local copies, waits for them, and re-layouts, on_device(): text_tokens.reshape(tok_rows, columns, pair_count, feature_slice)  7.86 us
    dot_general x1, matrix products, on_device(): lax.dot_general(value_grad, w_own, (((1,), (1,)), ((), ())), preferred_el...  7.4 us
  transfers between devices with their start and end apart: 7, of which 5 were waited for; matrix products, arithmetic and copies ran while one was open for 20% of the time, Pallas kernels for 0%

commit v1 on v0

v1 whole, which is shorter than its diff:
```python
import jax
import jax.numpy as jnp
from jax import lax
from jax.sharding import PartitionSpec as P

epsilon = 1e-05
f32 = jnp.float32
bf16 = jnp.bfloat16


def on_device(text_tokens, images, counts, offsets, norm_gain, value_weight, value_grad):
    sections = lax.axis_size("section")
    columns = lax.axis_size("fsdp")
    pairs = lax.axis_size("tp")
    tok_rows, width = text_tokens.shape
    tiles, slots, part = images.shape
    heads = value_grad.shape[1]
    group_rows = columns * tok_rows
    regions = group_rows // slots
    section = lax.axis_index("section")
    column = lax.axis_index("fsdp")
    pair = lax.axis_index("tp")

    meta = lax.all_gather(jnp.stack([offsets, counts]), "section", axis=0)
    all_off, all_cnt = meta[:, 0], meta[:, 1]
    w_own = lax.all_gather(value_weight, "section", axis=1, tiled=True)
    w_all = lax.all_gather(w_own, "fsdp", axis=0, tiled=True)
    grad_group = lax.all_gather(value_grad, "fsdp", axis=0, tiled=True)

    here = (all_off // group_rows) == section
    start_here = jnp.sum(jnp.where(here, all_off - section * group_rows, 0), axis=1)
    count_here = jnp.sum(jnp.where(here, all_cnt, 0), axis=1)
    slot_ids = jnp.arange(slots, dtype=jnp.int32)
    rows_here = jnp.where(
        slot_ids[None, :] < count_here[:, None], start_here[:, None] + slot_ids[None, :], -1
    ).reshape(-1)
    group_ids = jnp.arange(group_rows, dtype=jnp.int32)
    select_here = (rows_here[:, None] == group_ids[None, :]).astype(bf16)
    grad_out = jnp.dot(select_here, grad_group, preferred_element_type=f32).astype(bf16)
    grad_in = lax.all_to_all(
        grad_out.reshape(sections, slots, heads), "section", split_axis=0, concat_axis=0, tiled=True
    )
    target = offsets // group_rows
    route = (target[:, None] == jnp.arange(sections, dtype=jnp.int32)[None, :]).astype(bf16)
    grad_slots = jnp.einsum("kt,tjc->kjc", route, grad_in, preferred_element_type=f32).astype(bf16)
    grad_slots = grad_slots.reshape(tiles * slots, heads)

    flat = images.reshape(tiles * slots, part)
    flat_f = flat.astype(f32)
    square_sum = lax.psum(jnp.sum(flat_f * flat_f, axis=1), ("fsdp", "tp"))
    inv_rms = lax.rsqrt(square_sum / width + epsilon)[:, None]

    own = (column * pairs + pair) * part
    gain_part = lax.dynamic_slice_in_dim(norm_gain, own, part)
    w_gain = (w_own.astype(f32) * gain_part[:, None]).astype(bf16)
    product = jnp.dot(flat, w_gain, preferred_element_type=f32)
    inner = lax.psum(jnp.sum(product * grad_slots.astype(f32), axis=1), ("fsdp", "tp"))[:, None]
    grad_normed = lax.dot_general(
        grad_slots, w_own, (((1,), (1,)), ((), ())), preferred_element_type=f32
    )
    visual_grads = (
        inv_rms * (grad_normed * gain_part) - flat_f * (inv_rms * inv_rms * inv_rms) * inner / width
    ).astype(bf16)
    valid = (slot_ids[None, :] < counts[:, None]).reshape(-1, 1)
    visual_grads = jnp.where(valid, visual_grads, 0).reshape(images.shape)

    scaled = (product * inv_rms).astype(bf16).reshape(tiles, slots, heads)
    out_parts = jnp.einsum("kt,kjc->tjc", route, scaled, preferred_element_type=f32).astype(bf16)
    in_parts = lax.all_to_all(out_parts, "section", split_axis=0, concat_axis=0, tiled=True)
    placed = lax.dot_general(
        select_here,
        in_parts.reshape(sections * slots, heads),
        (((0,), (0,)), ((), ())),
        preferred_element_type=f32,
    ).astype(bf16)
    by_column = lax.all_to_all(
        placed.reshape(columns, tok_rows, heads), "fsdp", split_axis=0, concat_axis=0, tiled=True
    )
    visual_part = jnp.sum(by_column.astype(f32), axis=0)

    row_ids = column * tok_rows + jnp.arange(tok_rows, dtype=jnp.int32)
    covered = jnp.any(rows_here[None, :] == row_ids[:, None], axis=1)[:, None]
    text_f = text_tokens.astype(f32)
    text_rms = lax.rsqrt(jnp.sum(text_f * text_f, axis=1, keepdims=True) / width + epsilon)
    text_own = jnp.concatenate(
        [
            lax.dynamic_slice_in_dim(text_tokens, (f * pairs + pair) * part, part, axis=1)
            for f in range(columns)
        ],
        axis=1,
    )
    gain_own = jnp.concatenate(
        [
            lax.dynamic_slice_in_dim(norm_gain, (f * pairs + pair) * part, part)
            for f in range(columns)
        ]
    )
    w_all_gain = (w_all.astype(f32) * gain_own[:, None]).astype(bf16)
    text_part = jnp.dot(text_own, w_all_gain, preferred_element_type=f32) * text_rms
    part_values = jnp.where(covered, visual_part, text_part)
    values = lax.psum_scatter(part_values, "tp", scatter_dimension=1, tiled=True).astype(bf16)
    return (values, visual_grads)


def solution(mesh):
    placed = (
        P(("section", "fsdp"), None),
        P("section", None, ("fsdp", "tp")),
        P("section"),
        P("section"),
        P(),
        P(("fsdp", "tp"), "section"),
        P(("section", "fsdp"), None),
    )
    return jax.shard_map(
        on_device,
        mesh=mesh,
        in_specs=placed,
        out_specs=(P(("section", "fsdp"), "tp"), P("section", None, ("fsdp", "tp"))),
        check_vma=False,
    )
```

time: 277 us -> 191 us (0.69)
  local copies, waits for them, and re-layouts: 37 us -> 8.5 us
  waiting for transfers between devices: 112 us -> 89.2 us
  blocking collectives: 54 us -> 42.9 us
  starting transfers between devices: 18 us -> 7.5 us
  other arithmetic: 12.9 us -> 5.5 us
  matrix products: 27.9 us -> 23.1 us
    all_to_all x4 -> x2, waiting for transfers between devices: 71.8 us -> 35.8 us  [the longest x1 21.9 us: on_device(): lax.all_to_all(placed.reshape(columns, tok_rows, heads), 'fsdp', split_ax...]
    all_to_all x1, blocking collectives: 49 us -> 16.9 us  [on_device(): lax.all_to_all(out_parts, 'section', split_axis=0, concat_axis=0, tiled=T...]
    all_gather x2 -> x3, waiting for transfers between devices: 25.2 us -> 44 us  [the longest x1 23.5 us: on_device(): grad_group = lax.all_gather(value_grad, 'fsdp', axis=0, tiled=True)]
    psum x1, blocking collectives: 4.92 us -> 20.9 us  [on_device(): square_sum = lax.psum(jnp.sum(flat_f * flat_f, axis=1), ('fsdp', 'tp'))]
    dynamic_slice x2, local copies, waits for them, and re-layouts: 16.6 us -> 3.14 us  [the longest x1 3.12 us: on_device(): lax.dynamic_slice_in_dim(text_tokens, (f * pairs + pair) * part, part, ax...]
    all_to_all x4 -> x2, starting transfers between devices: 18 us -> 7.17 us  [the longest x1 3.65 us: on_device(): lax.all_to_all(grad_out.reshape(sections, slots, heads), 'section', split...]
    reduce_scatter x1, waiting for transfers between devices: 14.2 us -> 8.1 us  [on_device(): lax.psum_scatter(part_values, 'tp', scatter_dimension=1, tiled=True)]
    reshape x2, local copies, waits for them, and re-layouts: 7.88 us -> 2.16 us  [on_device(): scaled = (product * inv_rms).astype(bf16).reshape(tiles, slots, heads)]
  transfers between devices with their start and end apart: 7 -> 6, of which waited for: 5 -> 5; matrix products, arithmetic and copies ran while one was open for 20% -> 16% of each run, Pallas kernels for 0% -> 0%
where the time goes in v1:
time: 191 us
  waiting for transfers between devices  89.2 us (47%)
  blocking collectives  42.9 us (22%)
  matrix products  23.1 us (12%)
  between operations  14 us (7%)
  local copies, waits for them, and re-layouts  8.5 us (4%)
  starting transfers between devices  7.5 us (4%)
  other arithmetic  5.5 us (3%)
    all_gather x1, waiting for transfers between devices, on_device(): grad_group = lax.all_gather(value_grad, 'fsdp', axis=0, tiled=True)  23.5 us
    all_to_all x1, waiting for transfers between devices, on_device(): lax.all_to_all(placed.reshape(columns, tok_rows, heads), 'fsdp', split_ax...  21.9 us
    psum x1, blocking collectives, on_device(): square_sum = lax.psum(jnp.sum(flat_f * flat_f, axis=1), ('fsdp', 'tp'))  20.9 us
    all_gather x1, waiting for transfers between devices, on_device(): w_own = lax.all_gather(value_weight, 'section', axis=1, tiled=True)  20.4 us
    all_to_all x1, blocking collectives, on_device(): lax.all_to_all(out_parts, 'section', split_axis=0, concat_axis=0, tiled=T...  16.9 us
    all_to_all x1, waiting for transfers between devices, on_device(): lax.all_to_all(grad_out.reshape(sections, slots, heads), 'section', split...  13.8 us
    reduce_scatter x1, waiting for transfers between devices, on_device(): lax.psum_scatter(part_values, 'tp', scatter_dimension=1, tiled=True)  8.1 us
    dot_general x1, matrix products, on_device(): jnp.dot(text_own, w_all_gain, preferred_element_type=f32) * text_rms  5.22 us
  transfers between devices with their start and end apart: 6, of which 5 were waited for; matrix products, arithmetic and copies ran while one was open for 16% of the time, Pallas kernels for 0%

profile of v1, /device:TPU:0, one launch (start us, length us, event | category | flops | bytes accessed | tf_op | source)
XLA Modules:
  0.0 190.7 jit_solution(3152542434380411342)
XLA Ops:
  7.2 0.0 all-gather.6.cloned.1.call-start
  7.2 0.7 all-gather.6.cloned.1.call-update
  7.9 0.0 all-gather.10.cloned.1.call-start
  7.9 0.7 all-gather.10.cloned.1.call-update
  8.6 0.0 all-gather.8.cloned.1.call-start
  8.7 20.4 %all-gather.6.cloned.1.call-done = bf16[1024,512]{1,0:T(8,128)(2,1)} async-done(((bf16[1024,128]{1,0:T(8,128)(2,1)}), bf16[1024,512]{1,0:T(8,128)(2,1)}) %all-gather.6.cloned.1.call-update) | async-done | bytes 1048592 | tf_op jit(solution)/shard_map/all_gather | solution.py:26
  29.1 0.0 all-gather.8.cloned.1.call-update
  29.2 0.7 add_bitcast_fusion
  29.8 5.1 %all-gather.1 = s32[4,2,4]{2,1,0:T(2,128)S(1)} all-gather(s32[1,2,4]{2,1,0:T(2,128)S(1)} %add_bitcast_fusion), channel_id=2, replica_groups=mesh['section'=4,'fsdp'=4,'tp'=2] {'section'}, dimensions={0}, use_global_device_ids=true | all-gather | bytes 160 | tf_op jit(solution)/shard_map/all_gather | solution.py:24
  34.9 0.2 select_reduce_fusion.1
  35.1 0.1 select_bitcast_fusion
  35.1 23.5 %all-gather.10.cloned.1.call-done = bf16[1024,512]{1,0:T(8,128)(2,1)} async-done(((bf16[256,512]{1,0:T(8,128)(2,1)}), bf16[1024,512]{1,0:T(8,128)(2,1)}) %all-gather.10.cloned.1.call-update) | async-done | bytes 1048592 | tf_op jit(solution)/shard_map/all_gather | solution.py:28
  58.7 3.6 %fusion.16 = bf16[1024,512]{1,0:T(8,128)(2,1)} fusion(bf16[1024,512]{1,0:T(8,128)(2,1)} %all-gather.10.cloned.1.call-done, s32[1024]{0:T(1024)S(1)} %bitcast.48), kind=kOutput, calls=%fused_computation.26 | convolution fusion | flops 1075314688 | bytes 2101248 | tf_op jit(solution)/shard_map/dot_general | solution.py:39
  62.3 3.6 %all-to-all-start.2 = ((bf16[4,256,512]{2,1,0:T(8,128)(2,1)}), bf16[4,256,512]{2,1,0:T(8,128)(2,1)S(1)}, u32[]{:S(2)}, u32[]{:S(2)}) async-start(bf16[4,256,512]{2,1,0:T(8,128)(2,1)} %bitcast.45), calls=%async_computation.3 | async-start | bytes 2097152 | tf_op jit(solution)/shard_map/all_to_all | solution.py:40
  66.0 0.0 copy-done.1
  66.0 0.5 multiply_reduce_fusion.1
  66.5 0.0 copy-done.6
  66.5 0.0 copy-done.7
  66.6 13.8 %all-to-all-done.2 = bf16[4,256,512]{2,1,0:T(8,128)(2,1)S(1)} async-done(((bf16[4,256,512]{2,1,0:T(8,128)(2,1)}), bf16[4,256,512]{2,1,0:T(8,128)(2,1)S(1)}, u32[]{:S(2)}, u32[]{:S(2)}) %all-to-all-start.2) | async-done | bytes 1048608 | tf_op jit(solution)/shard_map/all_to_all | solution.py:40
  80.4 1.9 %convolution_convert_fusion = bf16[4,256,512]{2,0,1:T(4,128)(2,1)} fusion(bf16[4,256,512]{2,1,0:T(8,128)(2,1)S(1)} %all-to-all-done.2, s32[4]{0:T(128)S(1)} %and_select_fusion), kind=kOutput, calls=%fused_computation.27 | convolution fusion | flops 4718608 | bytes 2097168 | tf_op jit(solution)/shard_map/kt,tjc->kjc/dot_general | solution.py:45
  82.3 2.7 %copy.27 = bf16[4,256,512]{1,0,2:T(4,128)(2,1)S(1)} copy(bf16[4,256,512]{2,0,1:T(4,128)(2,1)} %convolution_convert_fusion) | data formatting | bytes 2097152 | tf_op jit(solution)/shard_map/convert_element_type | solution.py:45
  85.1 0.2 copy.32
  85.3 0.0 copy-start.5
  85.3 3.5 %fusion.12 = (f32[1024]{0:T(1024)S(1)}, f32[512,1024]{1,0:T(8,128)S(1)}) fusion(bf16[1024,512]{0,1:T(8,128)(2,1)S(1)} %bitcast.43, bf16[1024,1024]{1,0:T(8,128)(2,1)} %bitcast.41, bf16[1024,512]{1,0:T(8,128)(2,1)S(1)} %copy-done.3, f32[1024]{0:T(1024)S(1)} %get-tuple-element.12), kind=kOutput, calls=%fused_computation.19 | convolution fusion | flops 1076886528 | bytes 6299648 | tf_op jit(solution)/shard_map/dot_general | solution.py:56
  88.9 0.0 copy-done.5
  88.9 20.9 %all-reduce = (f32[1024]{0:T(1024)S(1)}, f32[1024]{0:T(1024)S(1)}) all-reduce(f32[1024]{0:T(1024)S(1)} %bitcast.51, f32[1024]{0:T(1024)S(1)} %get-tuple-element.19), channel_id=1, replica_groups=mesh['section'=4,'fsdp'=4,'tp'=2] {'fsdp','tp'}, use_global_device_ids=true, to_apply=%region_4.5 | all-reduce | flops 2048 | bytes 16384 | tf_op jit(solution)/shard_map/psum | solution.py:50
  109.8 0.2 fusion.11
  110.1 0.8 reshape.125
  110.9 1.4 copy.24
  112.2 1.2 convolution_convert_fusion.1
  113.4 0.2 copy.25
  113.6 16.9 %all_to_all.15 = bf16[4,256,512]{2,1,0:T(8,128)(2,1)S(1)} all-to-all(bf16[4,256,512]{2,1,0:T(8,128)(2,1)S(1)} %copy.25), channel_id=1, replica_groups=mesh['section'=4,'fsdp'=4,'tp'=2] {'section'}, dimensions={0} | all-to-all | bytes 2097152 | tf_op jit(solution)/shard_map/all_to_all | solution.py:69
  130.5 2.6 %fusion.15 = bf16[1024,512]{1,0:T(8,128)(2,1)} fusion(bf16[1024,512]{1,0:T(8,128)(2,1)S(1)} %bitcast.46, s32[1024]{0:T(1024)S(1)} %bitcast.49), kind=kOutput, calls=%fused_computation.25 | convolution fusion | flops 1075314688 | bytes 2101248 | tf_op jit(solution)/shard_map/dot_general | solution.py:70
  133.1 3.5 %all-to-all-start.1 = ((bf16[4,256,512]{2,1,0:T(8,128)(2,1)}), bf16[4,256,512]{2,1,0:T(8,128)(2,1)S(1)}, u32[]{:S(2)}, u32[]{:S(2)}) async-start(bf16[4,256,512]{2,1,0:T(8,128)(2,1)} %bitcast.9), calls=%async_computation.1 | async-start | bytes 2097152 | tf_op jit(solution)/shard_map/all_to_all | solution.py:76
  136.6 0.2 reduce-scatter.2.cloned.1.call-start
  136.9 0.0 copy-start
  136.9 0.3 compare_reduce_fusion
  137.2 3.1 %constant_dynamic-slice_fusion.3 = (bf16[256,1024]{1,0:T(8,128)(2,1)}, bf16[256,1024]{1,0:T(8,128)(2,1)}, bf16[256,1024]{1,0:T(8,128)(2,1)}, bf16[256,1024]{1,0:T(8,128)(2,1)}) fusion(bf16[256,8192]{1,0:T(8,128)(2,1)} %param.7, s32[]{:T(128)S(6)} %select_n.66, s32[]{:T(128)S(6)} %select_n.68, s32[]{:T(128)S(6)} %select_n.67, s32[]{:T(128)S(6)} %select_n.69), kind=kLoop, calls=%fused_computation.65 | loop fusion | bytes 4194320 | tf_op jit(solution)/shard_map/dynamic_slice | solution.py:87
  140.3 0.0 copy-done
  140.3 0.9 multiply_reduce_fusion
  141.2 21.9 %all-to-all-done.1 = bf16[4,256,512]{2,1,0:T(8,128)(2,1)S(1)} async-done(((bf16[4,256,512]{2,1,0:T(8,128)(2,1)}), bf16[4,256,512]{2,1,0:T(8,128)(2,1)S(1)}, u32[]{:S(2)}, u32[]{:S(2)}) %all-to-all-start.1) | async-done | bytes 1048608 | tf_op jit(solution)/shard_map/all_to_all | solution.py:76
  163.1 0.9 convert_reduce_fusion
  164.1 5.2 %fusion.20 = f32[256,512]{1,0:T(8,128)} fusion(f32[256,512]{1,0:T(8,128)} %convert_reduce_fusion, bf16[4096,512]{1,0:T(8,128)(2,1)} %all-gather.8.cloned.1.call-done, f32[4096]{0:T(1024)S(1)} %pad_maximum_fusion, bf16[256,1024]{1,0:T(8,128)(2,1)} %get-tuple-element.9, bf16[256,1024]{1,0:T(8,128)(2,1)} %get-tuple-element.7, ...), kind=kOutput, calls=%fused_computation.30 | convolution fusion | flops 1088684032 | bytes 7357696 | tf_op jit(solution)/shard_map/dot_general | solution.py:99
  169.3 0.0 reduce-scatter.2.cloned.1.call-update
  169.3 0.1 iota_compare_fusion.7
  169.4 5.0 %broadcast_select_fusion = bf16[1024,1024]{1,0:T(8,128)(2,1)} fusion(pred[1024]{0:T(1024)(128)(4,1)S(1)} %lt.75, f32[1024]{0:T(1024)S(1)} %get-tuple-element.5, f32[1024]{0:T(1024)S(1)} %get-tuple-element.15, bf16[1024,1024]{1,0:T(8,128)(2,1)S(1)} %bitcast.42, f32[1024]{0:T(1024)S(1)} %get-tuple-element.12, bf16[1024,512]{0,1:T(8,128)(2,1)} %bitcast.44, ...), kind=kOutput, calls=%fused_computation.24 | convolution fusion | flops 1083179008 | bytes 6308864 | tf_op jit(solution)/shard_map/dot_general | solution.py:58
  174.4 8.1 %reduce-scatter.2.cloned.1.call-done = f32[256,256]{1,0:T(8,128)} async-done(((f32[256,512]{1,0:T(8,128)}), f32[256,256]{1,0:T(8,128)}) %reduce-scatter.2.cloned.1.call-update) | async-done | bytes 262160 | tf_op jit(solution)/shard_map/reduce_scatter | solution.py:101
  182.5 1.6 convert_element_type.62
  (22 shorter events, 0.1 us)
Async XLA Ops:
  7.2 22.0 %all-gather.6.cloned.1.call-start = ((), (), s32[]{:S(2)}) async-start(), calls=%async_computation.4 | async-start | bytes 1310720 | tf_op jit(solution)/shard_map/all_gather | solution.py:26
  7.9 50.8 %all-gather.10.cloned.1.call-start = ((), (), s32[]{:S(2)}) async-start(), calls=%async_computation.7 | async-start | bytes 1310720 | tf_op jit(solution)/shard_map/all_gather | solution.py:28
  8.6 155.4 %all-gather.8.cloned.1.call-start = ((), (), s32[]{:S(2)}) async-start(), calls=%async_computation.5 | async-start | bytes 5242880 | tf_op jit(solution)/shard_map/all_gather | solution.py:27
  58.7 7.3 %copy-start.1 = (bf16[4,256,1024]{2,1,0:T(8,128)(2,1)S(1)}, bf16[4,256,1024]{2,1,0:T(8,128)(2,1)}, u32[]{:S(2)}) copy-start(bf16[4,256,1024]{2,1,0:T(8,128)(2,1)} %param.8) | copy-start | bytes 6291460
  62.3 4.2 %copy-start.6 = (f32[8192]{0:T(1024)S(1)}, f32[8192]{0:T(1024)}, u32[]{:S(2)}) copy-start(f32[8192]{0:T(1024)} %param.11) | copy-start | bytes 98308
  62.3 4.2 %copy-start.7 = (s32[4]{0:T(128)S(1)}, s32[4]{0:T(128)}, u32[]{:S(2)}) copy-start(s32[4]{0:T(128)} %param.10) | copy-start | bytes 52
  62.3 18.1 %all-to-all-start.2 = ((bf16[4,256,512]{2,1,0:T(8,128)(2,1)}), bf16[4,256,512]{2,1,0:T(8,128)(2,1)S(1)}, u32[]{:S(2)}, u32[]{:S(2)}) async-start(bf16[4,256,512]{2,1,0:T(8,128)(2,1)} %bitcast.45), calls=%async_computation.3 | async-start | bytes 2097152 | tf_op jit(solution)/shard_map/all_to_all | solution.py:40
  66.5 18.8 %copy-start.3 = (bf16[1024,512]{1,0:T(8,128)(2,1)S(1)}, bf16[1024,512]{1,0:T(8,128)(2,1)}, u32[]{:S(2)}) copy-start(bf16[1024,512]{1,0:T(8,128)(2,1)} %all-gather.6.cloned.1.call-done) | copy-start | bytes 3145732
  85.3 3.6 %copy-start.5 = (bf16[64,8,4,256]{3,1,2,0:T(8,128)(2,1)}, bf16[64,8,4,256]{3,1,2,0:T(8,128)(2,1)S(1)}, u32[]{:S(2)}) copy-start(bf16[64,8,4,256]{3,1,2,0:T(8,128)(2,1)S(1)} %copy.32) | copy-start | bytes 3145732
  133.1 30.0 %all-to-all-start.1 = ((bf16[4,256,512]{2,1,0:T(8,128)(2,1)}), bf16[4,256,512]{2,1,0:T(8,128)(2,1)S(1)}, u32[]{:S(2)}, u32[]{:S(2)}) async-start(bf16[4,256,512]{2,1,0:T(8,128)(2,1)} %bitcast.9), calls=%async_computation.1 | async-start | bytes 2097152 | tf_op jit(solution)/shard_map/all_to_all | solution.py:76
  136.6 45.9 %reduce-scatter.2.cloned.1.call-start = ((), (), s32[]{:S(2)}) async-start(), calls=%async_computation.6 | async-start | bytes 786432 | tf_op jit(solution)/shard_map/reduce_scatter | solution.py:101
  136.9 3.4 %copy-start = (bf16[256,8192]{1,0:T(8,128)(2,1)S(1)}, bf16[256,8192]{1,0:T(8,128)(2,1)}, u32[]{:S(2)}) copy-start(bf16[256,8192]{1,0:T(8,128)(2,1)} %param.7) | copy-start | bytes 12582916
  164.1 5.3 %copy-start.8 = (s32[4]{0:T(128)S(1)}, s32[4]{0:T(128)}, u32[]{:S(2)}) copy-start(s32[4]{0:T(128)} %param.9) | copy-start | bytes 52
  164.1 5.3 %copy-start.2 = (bf16[4,256,1024]{2,1,0:T(8,128)(2,1)S(1)}, bf16[4,256,1024]{2,1,0:T(8,128)(2,1)}, u32[]{:S(2)}) copy-start(bf16[4,256,1024]{2,1,0:T(8,128)(2,1)} %param.8) | copy-start | bytes 6291460
  164.1 5.3 %copy-start.4 = (bf16[1024,512]{1,0:T(8,128)(2,1)S(1)}, bf16[1024,512]{1,0:T(8,128)(2,1)}, u32[]{:S(2)}) copy-start(bf16[1024,512]{1,0:T(8,128)(2,1)} %all-gather.6.cloned.1.call-done) | copy-start | bytes 3145732
Sparse Core Ops, SparseCore 0:
  9.5 19.5 all-gather.5
  30.7 27.9 all-gather.9
  60.2 81.1 all-gather.7
  169.5 13.0 reduce-scatter.1

commit v2 on v1

v2 whole, which is shorter than its diff:
```python
import functools

import jax
import jax.numpy as jnp
from jax import lax
from jax.experimental import pallas as pl
from jax.experimental.pallas import tpu as pltpu
from jax.sharding import PartitionSpec as P

epsilon = 1e-05
f32 = jnp.float32
bf16 = jnp.bfloat16
MESH = pl.DeviceIdType.MESH


def kernel(
    width,
    a_tab,
    b_tab,
    r_tab,
    vg_ref,
    img_ref,
    sq_ref,
    wt_ref,
    grads,
    vis_ref,
    sqt_ref,
    inner_ref,
    wown,
    gath,
    gout,
    gin,
    ghalf,
    prod,
    pout,
    pin,
    psum,
    bout,
    bin_,
    cout,
    cin,
    sqbuf,
    innbuf,
    innown,
    s_vg,
    r_vg,
    s_w,
    r_w,
    s_sq,
    r_sq,
    s_a2,
    r_a2,
    s_a3,
    r_a3,
    s_b1,
    r_b1,
    s_b2,
    r_b2,
    s_b3,
    r_b3,
    s_in,
    r_in,
):
    sections, slots, half = gout.shape
    columns, tok, _ = cin.shape
    pairs = pout.shape[0]
    rows = psum.shape[0]
    tiles = rows // slots
    cols = wt_ref.shape[0]
    me_s, me_f, me_t = (lax.axis_index(n) for n in ("section", "fsdp", "tp"))
    others_s = [lax.rem(me_s + d, sections) for d in range(1, sections)]
    others_f = [lax.rem(me_f + d, columns) for d in range(1, columns)]
    others_t = [lax.rem(me_t + d, pairs) for d in range(1, pairs)]
    group = columns * pairs
    me_g = me_f * pairs + me_t
    others_g = [lax.rem(me_g + d, group) for d in range(1, group)]

    def on_s(s):
        return (s, me_f, me_t)

    def on_f(f):
        return (me_s, f, me_t)

    def on_t(t):
        return (me_s, me_f, t)

    def on_g(g):
        return (me_s, g // pairs, lax.rem(g, pairs))

    def copy(src, dst, s, r, dev):
        return pltpu.make_async_remote_copy(
            src_ref=src, dst_ref=dst, send_sem=s, recv_sem=r, device_id=dev, device_id_type=MESH
        )

    barrier = pltpu.get_barrier_semaphore()
    peers = [on_s(s) for s in others_s] + [on_g(g) for g in others_g]
    for dev in peers:
        pl.semaphore_signal(barrier, inc=1, device_id=dev, device_id_type=MESH)
    pl.semaphore_wait(barrier, len(peers))

    def slot(i, n):
        return pl.ds(pl.multiple_of(i * n, n), n)

    sent = []

    def send(src, dst, s, r, dev):
        c = copy(src, dst, s, r, dev)
        c.start()
        sent.append(c)

    for g in others_g:
        send(sq_ref, sqbuf.at[me_g], s_sq.at[g], r_sq.at[me_g], on_g(g))
    for s in others_s:
        send(wt_ref, wown.at[slot(me_s, cols)], s_w.at[s], r_w.at[me_s], on_s(s))
    for f in others_f:
        send(vg_ref, gath.at[slot(me_f, tok)], s_vg.at[f], r_vg.at[me_f], on_f(f))
    gath[slot(me_f, tok)] = vg_ref[...]
    wown[slot(me_s, cols)] = wt_ref[...]
    sqbuf[me_g] = sq_ref[...]

    def one_hot(n, m, start, lo, hi):
        r = lax.broadcasted_iota(jnp.int32, (n, m), 0)
        c = lax.broadcasted_iota(jnp.int32, (n, m), 1)
        hit = (c - r == start) & (r >= lo) & (r < hi)
        return jnp.where(hit, 1.0, 0.0).astype(bf16)

    def pick(n, start, lo, hi, ref):
        m = ref.shape[0]
        return jnp.dot(
            one_hot(n, m, start, lo, hi), ref[...], preferred_element_type=f32
        ).astype(bf16)

    for f in others_f:
        copy(vg_ref, gath.at[slot(f, tok)], s_vg.at[f], r_vg.at[f], on_f(f)).wait_recv()
    for s in others_s + [me_s]:
        block = pick(slots, a_tab[0, s], 0, a_tab[1, s], gath)
        if s is me_s:
            gin[slot(s, slots)] = block
        else:
            gout[s] = block
            send(gout.at[s], gin.at[slot(me_s, slots)], s_a2.at[s], r_a2.at[me_s], on_s(s))

    eye = lax.broadcasted_iota(jnp.int32, (128, 128), 0) == lax.broadcasted_iota(
        jnp.int32, (128, 128), 1
    )
    for g in others_g:
        copy(sq_ref, sqbuf.at[g], s_sq.at[g], r_sq.at[g], on_g(g)).wait_recv()
    total = jnp.sum(sqbuf[...], axis=0)
    sqt_ref[...] = total
    for s in others_s:
        copy(wt_ref, wown.at[slot(s, cols)], s_w.at[s], r_w.at[s], on_s(s)).wait_recv()

    def project(k, carry):
        at = slot(k, slots)
        p = lax.dot_general(
            img_ref[at], wown[...], (((1,), (1,)), ((), ())), preferred_element_type=f32
        )
        prod[at] = p
        for j in range(0, slots, 128):
            at_j = pl.ds(pl.multiple_of(k * slots + j, 128), 128)
            inv = lax.rsqrt(sqt_ref[:, at_j] / width + epsilon)
            inv = jnp.sum(jnp.where(eye, inv, 0.0), axis=1, keepdims=True)
            part = (p[j : j + 128] * inv).astype(bf16)
            for h in range(pairs):
                pout[h, at_j] = part[:, h * half : (h + 1) * half]
        return carry

    lax.fori_loop(0, tiles, project, 0)
    for t in others_t:
        send(pout.at[t], pin.at[me_t], s_b1.at[t], r_b1.at[me_t], on_t(t))
    pin[me_t] = pout[me_t]

    for s in others_s:
        copy(gout.at[s], gin.at[slot(s, slots)], s_a2.at[s], r_a2.at[s], on_s(s)).wait_recv()

    def order(k, carry):
        ghalf[slot(k, slots)] = pick(slots, r_tab[0, k], 0, slots, gin)
        return carry

    lax.fori_loop(0, tiles, order, 0)
    for t in others_t:
        send(ghalf, grads.at[me_t], s_a3.at[t], r_a3.at[me_t], on_t(t))
    grads[me_t] = ghalf[...]

    for t in others_t:
        copy(pout.at[t], pin.at[t], s_b1.at[t], r_b1.at[t], on_t(t)).wait_recv()
    acc = pin[0].astype(f32)
    for t in range(1, pairs):
        acc = acc + pin[t].astype(f32)
    psum[...] = acc.astype(bf16)
    for s in others_s + [me_s]:
        block = pick(slots, r_tab[1, s], 0, slots, psum)
        if s is me_s:
            bin_[slot(s, slots)] = block
        else:
            bout[s] = block
            send(bout.at[s], bin_.at[slot(me_s, slots)], s_b2.at[s], r_b2.at[me_s], on_s(s))

    for t in others_t:
        copy(ghalf, grads.at[t], s_a3.at[t], r_a3.at[t], on_t(t)).wait_recv()

    def dots(k, carry):
        at = pl.ds(pl.multiple_of(k * 128, 128), 128)
        s = jnp.zeros((128, half), f32)
        for h in range(pairs):
            s = s + prod[at, h * half : (h + 1) * half] * grads[h, at].astype(f32)
        col = jnp.sum(s, axis=1, keepdims=True)
        innown[:, at] = jnp.sum(jnp.where(eye, col, 0.0), axis=0, keepdims=True)
        return carry

    lax.fori_loop(0, rows // 128, dots, 0)
    for g in others_g:
        send(innown, innbuf.at[me_g], s_in.at[g], r_in.at[me_g], on_g(g))
    innbuf[me_g] = innown[...]

    for s in others_s:
        copy(bout.at[s], bin_.at[slot(s, slots)], s_b2.at[s], r_b2.at[s], on_s(s)).wait_recv()
    for f in others_f + [me_f]:
        base = lax.rem(f * tok, slots)
        r = (f * tok) // slots
        block = pick(tok, b_tab[0, r] + base, b_tab[1, r] - base, b_tab[2, r] - base, bin_)
        if f is me_f:
            cin[f] = block
        else:
            cout[f] = block
            send(cout.at[f], cin.at[me_f], s_b3.at[f], r_b3.at[me_f], on_f(f))
    for g in others_g:
        copy(innown, innbuf.at[g], s_in.at[g], r_in.at[g], on_g(g)).wait_recv()
    inner_ref[...] = jnp.sum(innbuf[...], axis=0)
    for f in others_f:
        copy(cout.at[f], cin.at[f], s_b3.at[f], r_b3.at[f], on_f(f)).wait_recv()
    acc = cin[0].astype(f32)
    for f in range(1, columns):
        acc = acc + cin[f].astype(f32)
    vis_ref[...] = acc
    for c in sent:
        c.wait_send()


def exchange(a_tab, b_tab, r_tab, vg_half, img_gain, squares, w_t, dims, width):
    sections, columns, pairs = dims
    tok, half = vg_half.shape
    rows, part = img_gain.shape
    slots = rows // r_tab.shape[1]
    heads = half * pairs
    group = columns * pairs
    vmem = pl.BlockSpec(memory_space=pltpu.VMEM)
    smem = pl.BlockSpec(memory_space=pltpu.SMEM)
    sems = []
    for n in (columns, sections, group, sections, pairs, pairs, sections, columns, group):
        sems += [pltpu.SemaphoreType.DMA((n,))] * 2
    return pl.pallas_call(
        functools.partial(kernel, width),
        out_shape=(
            jax.ShapeDtypeStruct((pairs, rows, half), bf16),
            jax.ShapeDtypeStruct((tok, half), f32),
            jax.ShapeDtypeStruct((1, rows), f32),
            jax.ShapeDtypeStruct((1, rows), f32),
            jax.ShapeDtypeStruct((heads, part), bf16),
        ),
        in_specs=[smem] * 3 + [vmem] * 4,
        out_specs=(vmem,) * 5,
        scratch_shapes=[
            pltpu.VMEM((columns * tok, half), bf16),
            pltpu.VMEM((sections, slots, half), bf16),
            pltpu.VMEM((sections * slots, half), bf16),
            pltpu.VMEM((rows, half), bf16),
            pltpu.VMEM((rows, heads), f32),
            pltpu.VMEM((pairs, rows, half), bf16),
            pltpu.VMEM((pairs, rows, half), bf16),
            pltpu.VMEM((rows, half), bf16),
            pltpu.VMEM((sections, slots, half), bf16),
            pltpu.VMEM((sections * slots, half), bf16),
            pltpu.VMEM((columns, tok, half), bf16),
            pltpu.VMEM((columns, tok, half), bf16),
            pltpu.VMEM((group, 1, rows), f32),
            pltpu.VMEM((group, 1, rows), f32),
            pltpu.VMEM((1, rows), f32),
        ]
        + sems,
        compiler_params=pltpu.CompilerParams(
            collective_id=0, has_side_effects=True, vmem_limit_bytes=56 * 1024 * 1024
        ),
        cost_estimate=pl.CostEstimate(
            flops=40 * rows * part * heads, bytes_accessed=64 * rows * heads, transcendentals=0
        ),
    )(a_tab, b_tab, r_tab, vg_half, img_gain, squares, w_t)


def on_device(text_tokens, images, counts, offsets, norm_gain, value_weight, value_grad):
    sections = lax.axis_size("section")
    columns = lax.axis_size("fsdp")
    pairs = lax.axis_size("tp")
    tok_rows, width = text_tokens.shape
    tiles, slots, part = images.shape
    heads = value_grad.shape[1]
    half = heads // pairs
    group_rows = columns * tok_rows
    regions = group_rows // slots
    section = lax.axis_index("section")
    column = lax.axis_index("fsdp")
    pair = lax.axis_index("tp")

    meta = lax.all_gather(jnp.stack([offsets, counts]), "section", axis=0)
    all_off, all_cnt = meta[:, 0], meta[:, 1]
    w_rows = lax.all_gather(value_weight, "fsdp", axis=0, tiled=True)
    w_all = lax.all_gather(w_rows, "section", axis=1, tiled=True)

    here = (all_off // group_rows) == section
    start_here = jnp.sum(jnp.where(here, all_off - section * group_rows, 0), axis=1)
    count_here = jnp.sum(jnp.where(here, all_cnt, 0), axis=1)
    a_tab = jnp.stack([start_here, count_here])
    region_here = start_here // slots
    first_here = start_here % slots
    source_ids = jnp.arange(sections, dtype=jnp.int32)
    region_ids = jnp.arange(regions, dtype=jnp.int32)
    holds = region_here[None, :] == region_ids[:, None]
    by_region = jnp.stack([source_ids * slots - first_here, first_here, first_here + count_here])
    b_tab = jnp.sum(jnp.where(holds[None], by_region[:, None, :], 0), axis=2)
    target = offsets // group_rows
    tile_ids = jnp.arange(tiles, dtype=jnp.int32)
    inverse = jnp.sum(
        jnp.where(target[None, :] == source_ids[:, None], tile_ids[None, :], 0), axis=1
    )
    r_tab = jnp.stack([target, inverse]) * slots

    own = (column * pairs + pair) * part
    gain_part = lax.dynamic_slice_in_dim(norm_gain, own, part)
    flat = images.reshape(tiles * slots, part)
    flat_f = flat.astype(f32)
    img_gain = (flat_f * gain_part).astype(bf16)
    squares = jnp.sum(flat_f * flat_f, axis=1)[None, :]
    vg_half = lax.dynamic_slice_in_dim(value_grad, pair * half, half, axis=1)
    grads, visual, square_sum, inner, w_own_t = exchange(
        a_tab,
        b_tab,
        r_tab,
        vg_half,
        img_gain,
        squares,
        value_weight.T,
        (sections, columns, pairs),
        width,
    )
    square_sum = square_sum.reshape(-1, 1)
    inner = inner.reshape(-1, 1)
    inv_rms = lax.rsqrt(square_sum / width + epsilon)
    grad_normed = sum(
        jnp.dot(grads[h], w_own_t[h * half : (h + 1) * half], preferred_element_type=f32)
        for h in range(pairs)
    )
    visual_grads = (
        inv_rms * (grad_normed * gain_part) - flat_f * (inv_rms * inv_rms * inv_rms) * inner / width
    ).astype(bf16)
    slot_ids = jnp.arange(slots, dtype=jnp.int32)
    valid = (slot_ids[None, :] < counts[:, None]).reshape(-1, 1)
    visual_grads = jnp.where(valid, visual_grads, 0).reshape(images.shape)

    first_row = column * tok_rows
    local = first_row % slots + jnp.arange(tok_rows, dtype=jnp.int32)
    bounds = lax.dynamic_index_in_dim(b_tab, first_row // slots, 1, keepdims=False)
    covered = ((local >= bounds[1]) & (local < bounds[2]))[:, None]
    text_f = text_tokens.astype(f32)
    text_rms = lax.rsqrt(jnp.sum(text_f * text_f, axis=1, keepdims=True) / width + epsilon)
    text_own = jnp.concatenate(
        [
            lax.dynamic_slice_in_dim(text_tokens, (f * pairs + pair) * part, part, axis=1)
            for f in range(columns)
        ],
        axis=1,
    )
    gain_own = jnp.concatenate(
        [
            lax.dynamic_slice_in_dim(norm_gain, (f * pairs + pair) * part, part)
            for f in range(columns)
        ]
    )
    text_gain = (text_own.astype(f32) * gain_own).astype(bf16)
    text_part = jnp.dot(text_gain, w_all, preferred_element_type=f32) * text_rms
    text_values = lax.psum_scatter(text_part, "tp", scatter_dimension=1, tiled=True)
    values = jnp.where(covered, visual, text_values).astype(bf16)
    return (values, visual_grads)


def solution(mesh):
    placed = (
        P(("section", "fsdp"), None),
        P("section", None, ("fsdp", "tp")),
        P("section"),
        P("section"),
        P(),
        P(("fsdp", "tp"), "section"),
        P(("section", "fsdp"), None),
    )
    return jax.shard_map(
        on_device,
        mesh=mesh,
        in_specs=placed,
        out_specs=(P(("section", "fsdp"), "tp"), P("section", None, ("fsdp", "tp"))),
        check_vma=False,
    )
```

time: 191 us -> 150 us (0.79)
  Pallas kernels: 0 us -> 58.9 us
  waiting for transfers between devices: 89.2 us -> 41.8 us
  blocking collectives: 42.9 us -> 5.06 us
  matrix products: 23.1 us -> 9.66 us
  other arithmetic: 5.5 us -> 12.9 us
  starting transfers between devices: 7.5 us -> 0.12 us
    pallas_call x0 -> x1, Pallas kernels: none -> 58.9 us  [exchange(): pl.pallas_call(functools.partial(kernel, width), out_shape=(jax.ShapeDtyp...]
    all_to_all x2 -> x0, waiting for transfers between devices: 35.8 us -> none  [the longest x1 21.9 us: on_device(): lax.all_to_all(placed.reshape(columns, tok_rows, heads), 'fsdp', split_ax...]
    psum x1 -> x0, blocking collectives: 20.9 us -> none  [on_device(): square_sum = lax.psum(jnp.sum(flat_f * flat_f, axis=1), ('fsdp', 'tp'))]
    all_to_all x1 -> x0, blocking collectives: 16.9 us -> none  [on_device(): lax.all_to_all(out_parts, 'section', split_axis=0, concat_axis=0, tiled=T...]
    dot_general x7 -> x3, matrix products: 23.1 us -> 9.66 us  [the longest x1 4.97 us: on_device(): text_part = jnp.dot(text_gain, w_all, preferred_element_type=f32) * text_rms]
    all_gather x3 -> x2, waiting for transfers between devices: 44 us -> 31.6 us  [the longest x1 31.6 us: on_device(): w_rows = lax.all_gather(value_weight, 'fsdp', axis=0, tiled=True)]
    all_to_all x2 -> x0, starting transfers between devices: 7.17 us -> none  [the longest x1 3.65 us: on_device(): lax.all_to_all(grad_out.reshape(sections, slots, heads), 'section', split...]
    convert_element_type x2 -> x0, local copies, waits for them, and re-layouts: 2.93 us -> none  [the longest x1 2.73 us: on_device(): jnp.einsum('kt,tjc->kjc', route, grad_in, preferred_element_type=f32)]
  transfers between devices with their start and end apart: 6 -> 3, of which waited for: 5 -> 2; matrix products, arithmetic and copies ran while one was open for 16% -> 16% of each run, Pallas kernels for 0% -> 39%
where the time goes in v2:
time: 150 us
  Pallas kernels  58.9 us (39%)
  waiting for transfers between devices  41.8 us (28%)
  between operations  13.9 us (9%)
  other arithmetic  12.9 us (9%)
  matrix products  9.66 us (6%)
  local copies, waits for them, and re-layouts  7.59 us (5%)
  blocking collectives  5.06 us (3%)
    pallas_call x1, Pallas kernels, exchange(): pl.pallas_call(functools.partial(kernel, width), out_shape=(jax.ShapeDtyp...  58.9 us
    all_gather x1, waiting for transfers between devices, on_device(): w_rows = lax.all_gather(value_weight, 'fsdp', axis=0, tiled=True)  31.6 us
    reduce_scatter x1, waiting for transfers between devices, on_device(): lax.psum_scatter(text_part, 'tp', scatter_dimension=1, tiled=True)  9.45 us
    all_gather x1, blocking collectives, on_device(): meta = lax.all_gather(jnp.stack([offsets, counts]), 'section', axis=0)  5.06 us
    dot_general x1, matrix products, on_device(): text_part = jnp.dot(text_gain, w_all, preferred_element_type=f32) * text_rms  4.97 us
    dot_general x2, matrix products, on_device(): jnp.dot(grads[h], w_own_t[h * half:(h + 1) * half], preferred_element_typ...  4.69 us
    dynamic_slice x1, local copies, waits for them, and re-layouts, on_device(): lax.dynamic_slice_in_dim(text_tokens, (f * pairs + pair) * part, part, ax...  3.07 us
  transfers between devices with their start and end apart: 3, of which 2 were waited for; matrix products, arithmetic and copies ran while one was open for 16% of the time, Pallas kernels for 39%

profile of v2, /device:TPU:0, one launch (start us, length us, event | category | flops | bytes accessed | tf_op | source)
XLA Modules:
  0.0 149.9 jit_solution(5884236618733090780)
XLA Ops:
  7.2 0.0 copy-start
  7.2 0.0 all-gather.5.cloned.1.call-start
  7.2 0.7 all-gather.5.cloned.1.call-update
  7.9 0.0 all-gather.7.cloned.1.call-start
  8.0 0.7 add_bitcast_fusion
  8.6 31.6 %all-gather.5.cloned.1.call-done = bf16[4096,128]{1,0:T(8,128)(2,1)} async-done(((bf16[1024,128]{1,0:T(8,128)(2,1)}), bf16[4096,128]{1,0:T(8,128)(2,1)}) %all-gather.5.cloned.1.call-update) | async-done | bytes 1048592 | tf_op jit(solution)/shard_map/all_gather | solution.py:306
  40.2 0.0 all-gather.7.cloned.1.call-update
  40.3 0.0 reduce-scatter.2.cloned.1.call-start
  40.3 0.7 iota_compare_fusion
  41.0 5.1 %all-gather.1 = s32[4,2,4]{2,1,0:T(2,128)S(1)} all-gather(s32[1,2,4]{2,1,0:T(2,128)S(1)} %add_bitcast_fusion), channel_id=2, replica_groups=mesh['section'=4,'fsdp'=4,'tp'=2] {'section'}, dimensions={0}, use_global_device_ids=true | all-gather | bytes 160 | tf_op jit(solution)/shard_map/all_gather | solution.py:304
  46.1 1.8 %copy.11 = bf16[1024,128]{0,1:T(8,128)(2,1)} copy(bf16[1024,128]{1,0:T(8,128)(2,1)} %param.12) | data formatting | bytes 524288 | tf_op args[5]
  47.9 2.3 %fusion = f32[4,256]{1,0:T(4,128)S(1)} fusion(bf16[4,256,1024]{2,1,0:T(8,128)(2,1)} %param.8), kind=kLoop, calls=%fused_computation.4 | loop fusion | flops 3144704 | bytes 2101248 | tf_op jit(solution)/shard_map/reduce_sum | solution.py:332
  50.2 0.6 copy.12
  50.8 0.0 copy-start.1
  50.8 0.2 select_reduce_fusion.3
  51.0 0.1 select_reduce_fusion.b_tab
  51.2 0.0 copy-start.5
  51.2 0.1 constant_dynamic-slice_fusion.5
  51.3 0.9 and_select_fusion
  52.2 0.1 select_reduce_fusion.1
  52.3 0.7 fusion.32
  53.0 0.6 pad_add_fusion.1
  53.6 0.5 fusion.30
  54.1 0.8 fusion.28
  54.9 0.0 copy-done
  54.9 0.7 constant_dynamic-slice_fusion.4.vg_ref
  55.6 3.1 %constant_dynamic-slice_fusion.3 = (bf16[256,1024]{1,0:T(8,128)(2,1)}, bf16[256,1024]{1,0:T(8,128)(2,1)}, bf16[256,1024]{1,0:T(8,128)(2,1)}, bf16[256,1024]{1,0:T(8,128)(2,1)}) fusion(bf16[256,8192]{1,0:T(8,128)(2,1)} %param.7, s32[]{:T(128)S(6)} %select_n.111, s32[]{:T(128)S(6)} %select_n.113, s32[]{:T(128)S(6)} %select_n.112, s32[]{:T(128)S(6)} %select_n.114), kind=kLoop, calls=%fused_computation.58 | loop fusion | bytes 4194320 | tf_op jit(solution)/shard_map/dynamic_slice | solution.py:367
  58.7 0.0 copy-done.1
  58.7 0.9 multiply_reduce_fusion
  59.6 0.0 copy-done.5
  59.6 0.0 copy-done.2
  59.6 1.9 %fusion.1.img_ref = bf16[1024,1024]{1,0:T(8,128)(2,1)} fusion(bf16[4,256,1024]{2,1,0:T(8,128)(2,1)S(1)} %copy-done.2, f32[1024]{0:T(1024)S(1)} %get-tuple-element.20), kind=kLoop, calls=%fused_computation.5 | loop fusion | flops 3145728 | bytes 4198400 | tf_op jit(solution)/shard_map/convert_element_type | solution.py:331
  61.5 58.9 %shard_map.86 = (bf16[2,1024,256]{2,1,0:T(8,128)(2,1)}, f32[256,256]{1,0:T(8,128)}, f32[1,1024]{1,0:T(1,128)}, f32[1,1024]{1,0:T(1,128)}, bf16[512,1024]{1,0:T(8,128)(2,1)}) custom-call(s32[2,4]{1,0:T(2,128)} %get-tuple-element.30.a_tab, s32[3,4]{1,0:T(4,128)} %copy-done.5, s32[2,4]{1,0:T(2,128)} %get-tuple-element.31.r_tab, ...), custom_call_target="tpu_custom_call" | custom-call | flops 21474836480 | bytes 33554432 | tf_op jit(solution)/shard_map/pallas_call | solution.py:252
  120.4 0.7 add_rsqrt_fusion
  121.1 0.0 all-gather.7.cloned.1.call-done
  121.2 0.0 copy-start.3
  121.2 5.0 %fusion.15 = f32[256,512]{1,0:T(8,128)} fusion(bf16[4096,512]{1,0:T(8,128)(2,1)} %all-gather.7.cloned.1.call-done, bf16[256,1024]{1,0:T(8,128)(2,1)} %get-tuple-element.17, bf16[256,1024]{1,0:T(8,128)(2,1)} %get-tuple-element.15, bf16[256,1024]{1,0:T(8,128)(2,1)} %get-tuple-element.16, bf16[256,1024]{1,0:T(8,128)(2,1)} %get-tuple-element.14, ...), kind=kOutput, calls=%fused_computation.21 | convolution fusion | flops 1084358656 | bytes 6833152 | tf_op jit(solution)/shard_map/dot_general | solution.py:379
  126.1 0.0 reduce-scatter.2.cloned.1.call-update
  126.2 1.2 compare_and_fusion
  127.4 0.0 copy-done.3
  127.4 0.0 copy-start.4
  127.4 0.0 copy-start.6
  127.4 1.8 %fusion.17 = f32[1024,1024]{1,0:T(8,128)S(1)} fusion(bf16[512,1024]{1,0:T(8,128)(2,1)} %get-tuple-element.10, bf16[2,1024,256]{2,1,0:T(8,128)(2,1)S(1)} %copy-done.3), kind=kOutput, calls=%fused_computation.23 | convolution fusion | flops 536870912 | bytes 5242880 | tf_op jit(solution)/shard_map/dot_general | solution.py:349
  129.3 0.0 copy-done.4
  129.3 0.0 copy-done.6
  129.3 2.8 %broadcast_select_fusion = bf16[1024,1024]{1,0:T(8,128)(2,1)} fusion(pred[1024]{0:T(1024)(128)(4,1)S(1)} %lt.82, f32[1024]{0:T(1024)S(1)} %bitcast.61, f32[1024]{0:T(1024)S(1)} %multiply_multiply_fusion, bf16[4,256,1024]{2,1,0:T(8,128)(2,1)S(1)} %copy-done.2, f32[1024]{0:T(1024)S(1)} %get-tuple-element.20, f32[1024,1024]{1,0:T(8,128)S(1)} %fusion.17, ...), kind=kOutput, calls=%fused_computation.20 | convolution fusion | flops 547356672 | bytes 9454592 | tf_op jit(solution)/shard_map/dot_general | solution.py:349
  132.1 9.4 %reduce-scatter.2.cloned.1.call-done = f32[256,256]{1,0:T(8,128)} async-done(((f32[256,512]{1,0:T(8,128)}), f32[256,256]{1,0:T(8,128)}) %reduce-scatter.2.cloned.1.call-update) | async-done | bytes 262160 | tf_op jit(solution)/shard_map/reduce_scatter | solution.py:380
  141.6 1.8 %select_convert_fusion = bf16[256,256]{1,0:T(8,128)(2,1)} fusion(f32[256,256]{1,0:T(8,128)} %get-tuple-element.7, f32[256,256]{1,0:T(8,128)} %reduce-scatter.2.cloned.1.call-done, pred[256]{0:T(512)(128)(4,1)S(1)} %compare_and_fusion), kind=kLoop, calls=%fused_computation.29 | loop fusion | flops 65536 | bytes 655616 | tf_op jit(solution)/shard_map/convert_element_type | solution.py:381
  (10 shorter events, 0.1 us)
Async XLA Ops:
  7.2 47.8 %copy-start = (bf16[256,512]{1,0:T(8,128)(2,1)S(1)}, bf16[256,512]{1,0:T(8,128)(2,1)}, u32[]{:S(2)}) copy-start(bf16[256,512]{1,0:T(8,128)(2,1)} %param.13) | copy-start | bytes 786436
  7.2 33.1 %all-gather.5.cloned.1.call-start = ((), (), s32[]{:S(2)}) async-start(), calls=%async_computation.1 | async-start | bytes 1310720 | tf_op jit(solution)/shard_map/all_gather | solution.py:306
  7.9 113.2 %all-gather.7.cloned.1.call-start = ((), (), s32[]{:S(2)}) async-start(), calls=%async_computation.2 | async-start | bytes 5242880 | tf_op jit(solution)/shard_map/all_gather | solution.py:307
  40.3 101.3 %reduce-scatter.2.cloned.1.call-start = ((), (), s32[]{:S(2)}) async-start(), calls=%async_computation.3 | async-start | bytes 786432 | tf_op jit(solution)/shard_map/reduce_scatter | solution.py:380
  50.8 7.8 %copy-start.1 = (bf16[256,8192]{1,0:T(8,128)(2,1)S(1)}, bf16[256,8192]{1,0:T(8,128)(2,1)}, u32[]{:S(2)}) copy-start(bf16[256,8192]{1,0:T(8,128)(2,1)} %param.7) | copy-start | bytes 12582916
  51.2 8.4 %copy-start.5 = (s32[3,4]{1,0:T(4,128)}, s32[3,4]{1,0:T(4,128)S(1)}, u32[]{:S(2)}) copy-start(s32[3,4]{1,0:T(4,128)S(1)} %select_reduce_fusion.b_tab) | copy-start | bytes 148
  55.6 4.0 %copy-start.2 = (bf16[4,256,1024]{2,1,0:T(8,128)(2,1)S(1)}, bf16[4,256,1024]{2,1,0:T(8,128)(2,1)}, u32[]{:S(2)}) copy-start(bf16[4,256,1024]{2,1,0:T(8,128)(2,1)} %param.8) | copy-start | bytes 6291460
  121.2 6.3 %copy-start.3 = (bf16[2,1024,256]{2,1,0:T(8,128)(2,1)S(1)}, bf16[2,1024,256]{2,1,0:T(8,128)(2,1)}, u32[]{:S(2)}) copy-start(bf16[2,1024,256]{2,1,0:T(8,128)(2,1)} %get-tuple-element.9) | copy-start | bytes 3145732
  127.4 1.9 %copy-start.4 = (bf16[512,1024]{1,0:T(8,128)(2,1)S(1)}, bf16[512,1024]{1,0:T(8,128)(2,1)}, u32[]{:S(2)}) copy-start(bf16[512,1024]{1,0:T(8,128)(2,1)} %get-tuple-element.10) | copy-start | bytes 3145732
  127.4 1.9 %copy-start.6 = (f32[1,1024]{1,0:T(1,128)S(1)}, f32[1,1024]{1,0:T(1,128)}, u32[]{:S(2)}) copy-start(f32[1,1024]{1,0:T(1,128)} %get-tuple-element.11) | copy-start | bytes 12292
Sparse Core Ops, SparseCore 0:
  9.6 30.6 all-gather.4
  41.8 40.0 all-gather.6
  126.3 15.2 reduce-scatter.1

commit v3 on v2

--- a/solution.py
+++ b/solution.py
@@ -108,10 +108,10 @@
         c.start()
         sent.append(c)
 
+    for s in others_s:
+        send(wt_ref, wown.at[slot(me_s, cols)], s_w.at[s], r_w.at[me_s], on_s(s))
     for g in others_g:
         send(sq_ref, sqbuf.at[me_g], s_sq.at[g], r_sq.at[me_g], on_g(g))
-    for s in others_s:
-        send(wt_ref, wown.at[slot(me_s, cols)], s_w.at[s], r_w.at[me_s], on_s(s))
     for f in others_f:
         send(vg_ref, gath.at[slot(me_f, tok)], s_vg.at[f], r_vg.at[me_f], on_f(f))
     gath[slot(me_f, tok)] = vg_ref[...]
@@ -129,16 +129,6 @@
         return jnp.dot(
             one_hot(n, m, start, lo, hi), ref[...], preferred_element_type=f32
         ).astype(bf16)
-
-    for f in others_f:
-        copy(vg_ref, gath.at[slot(f, tok)], s_vg.at[f], r_vg.at[f], on_f(f)).wait_recv()
-    for s in others_s + [me_s]:
-        block = pick(slots, a_tab[0, s], 0, a_tab[1, s], gath)
-        if s is me_s:
-            gin[slot(s, slots)] = block
-        else:
-            gout[s] = block
-            send(gout.at[s], gin.at[slot(me_s, slots)], s_a2.at[s], r_a2.at[me_s], on_s(s))
 
     eye = lax.broadcasted_iota(jnp.int32, (128, 128), 0) == lax.broadcasted_iota(
         jnp.int32, (128, 128), 1
@@ -163,12 +153,28 @@
             part = (p[j : j + 128] * inv).astype(bf16)
             for h in range(pairs):
                 pout[h, at_j] = part[:, h * half : (h + 1) * half]
+        for t in others_t:
+            tile_copy(t, me_t, k).start()
         return carry
 
+    def tile_copy(t, source, k):
+        at = slot(k, slots)
+        return copy(
+            pout.at[t, at], pin.at[source, at], s_b1.at[t, k], r_b1.at[source, k], on_t(t)
+        )
+
     lax.fori_loop(0, tiles, project, 0)
-    for t in others_t:
-        send(pout.at[t], pin.at[me_t], s_b1.at[t], r_b1.at[me_t], on_t(t))
     pin[me_t] = pout[me_t]
+
+    for f in others_f:
+        copy(vg_ref, gath.at[slot(f, tok)], s_vg.at[f], r_vg.at[f], on_f(f)).wait_recv()
+    for s in others_s + [me_s]:
+        block = pick(slots, a_tab[0, s], 0, a_tab[1, s], gath)
+        if s is me_s:
+            gin[slot(s, slots)] = block
+        else:
+            gout[s] = block
+            send(gout.at[s], gin.at[slot(me_s, slots)], s_a2.at[s], r_a2.at[me_s], on_s(s))
 
     for s in others_s:
         copy(gout.at[s], gin.at[slot(s, slots)], s_a2.at[s], r_a2.at[s], on_s(s)).wait_recv()
@@ -182,8 +188,12 @@
         send(ghalf, grads.at[me_t], s_a3.at[t], r_a3.at[me_t], on_t(t))
     grads[me_t] = ghalf[...]
 
-    for t in others_t:
-        copy(pout.at[t], pin.at[t], s_b1.at[t], r_b1.at[t], on_t(t)).wait_recv()
+    def arrived(k, carry):
+        for t in others_t:
+            tile_copy(t, t, k).wait_recv()
+        return carry
+
+    lax.fori_loop(0, tiles, arrived, 0)
     acc = pin[0].astype(f32)
     for t in range(1, pairs):
         acc = acc + pin[t].astype(f32)
@@ -236,6 +246,13 @@
     for c in sent:
         c.wait_send()
 
+    def left(k, carry):
+        for t in others_t:
+            tile_copy(t, me_t, k).wait_send()
+        return carry
+
+    lax.fori_loop(0, tiles, left, 0)
+
 
 def exchange(a_tab, b_tab, r_tab, vg_half, img_gain, squares, w_t, dims, width):
     sections, columns, pairs = dims
@@ -247,8 +264,9 @@
     vmem = pl.BlockSpec(memory_space=pltpu.VMEM)
     smem = pl.BlockSpec(memory_space=pltpu.SMEM)
     sems = []
-    for n in (columns, sections, group, sections, pairs, pairs, sections, columns, group):
-        sems += [pltpu.SemaphoreType.DMA((n,))] * 2
+    tiles = rows // slots
+    for n in (columns, sections, group, sections, pairs, (pairs, tiles), sections, columns, group):
+        sems += [pltpu.SemaphoreType.DMA(n if isinstance(n, tuple) else (n,))] * 2
     return pl.pallas_call(
         functools.partial(kernel, width),
         out_shape=(
@@ -303,8 +321,8 @@
 
     meta = lax.all_gather(jnp.stack([offsets, counts]), "section", axis=0)
     all_off, all_cnt = meta[:, 0], meta[:, 1]
-    w_rows = lax.all_gather(value_weight, "fsdp", axis=0, tiled=True)
-    w_all = lax.all_gather(w_rows, "section", axis=1, tiled=True)
+    w_all = lax.all_gather(value_weight, ("section", "fsdp"), axis=0, tiled=True)
+    w_all = w_all.reshape(sections, columns * part, -1)
 
     here = (all_off // group_rows) == section
     start_here = jnp.sum(jnp.where(here, all_off - section * group_rows, 0), axis=1)
@@ -342,20 +360,6 @@
         (sections, columns, pairs),
         width,
     )
-    square_sum = square_sum.reshape(-1, 1)
-    inner = inner.reshape(-1, 1)
-    inv_rms = lax.rsqrt(square_sum / width + epsilon)
-    grad_normed = sum(
-        jnp.dot(grads[h], w_own_t[h * half : (h + 1) * half], preferred_element_type=f32)
-        for h in range(pairs)
-    )
-    visual_grads = (
-        inv_rms * (grad_normed * gain_part) - flat_f * (inv_rms * inv_rms * inv_rms) * inner / width
-    ).astype(bf16)
-    slot_ids = jnp.arange(slots, dtype=jnp.int32)
-    valid = (slot_ids[None, :] < counts[:, None]).reshape(-1, 1)
-    visual_grads = jnp.where(valid, visual_grads, 0).reshape(images.shape)
-
     first_row = column * tok_rows
     local = first_row % slots + jnp.arange(tok_rows, dtype=jnp.int32)
     bounds = lax.dynamic_index_in_dim(b_tab, first_row // slots, 1, keepdims=False)
@@ -376,8 +380,25 @@
         ]
     )
     text_gain = (text_own.astype(f32) * gain_own).astype(bf16)
-    text_part = jnp.dot(text_gain, w_all, preferred_element_type=f32) * text_rms
+    text_part = text_rms * jnp.concatenate(
+        [jnp.dot(text_gain, w_all[s], preferred_element_type=f32) for s in range(sections)], axis=1
+    )
+    grads, text_part = lax.optimization_barrier((grads, text_part))
     text_values = lax.psum_scatter(text_part, "tp", scatter_dimension=1, tiled=True)
+    square_sum = square_sum.reshape(-1, 1)
+    inner = inner.reshape(-1, 1)
+    inv_rms = lax.rsqrt(square_sum / width + epsilon)
+    grad_normed = sum(
+        jnp.dot(grads[h], w_own_t[h * half : (h + 1) * half], preferred_element_type=f32)
+        for h in range(pairs)
+    )
+    visual_grads = (
+        inv_rms * (grad_normed * gain_part) - flat_f * (inv_rms * inv_rms * inv_rms) * inner / width
+    ).astype(bf16)
+    slot_ids = jnp.arange(slots, dtype=jnp.int32)
+    valid = (slot_ids[None, :] < counts[:, None]).reshape(-1, 1)
+    visual_grads = jnp.where(valid, visual_grads, 0).reshape(images.shape)
+
     values = jnp.where(covered, visual, text_values).astype(bf16)
     return (values, visual_grads)
 

time: 150 us -> 129 us (0.86)
  waiting for transfers between devices: 41.8 us -> 12 us
  Pallas kernels: 58.9 us -> 64.3 us
    all_gather x2 -> x1, waiting for transfers between devices: 31.6 us -> 0.02 us  [on_device(): lax.all_gather(value_weight, ('section', 'fsdp'), axis=0, tiled=True)]
    pallas_call x1, Pallas kernels: 58.9 us -> 64.3 us  [exchange(): pl.pallas_call(functools.partial(kernel, width), out_shape=(jax.ShapeDtyp...]
    reduce_scatter x1, waiting for transfers between devices: 9.45 us -> 11.3 us  [on_device(): lax.psum_scatter(text_part, 'tp', scatter_dimension=1, tiled=True)]
    dot_general x1 -> x4, matrix products: 4.97 us -> 5.83 us  [on_device(): jnp.dot(text_gain, w_all[s], preferred_element_type=f32)]
    unnamed x16 -> x26, local copies, waits for them, and re-layouts: 2.44 us -> 3.13 us
  transfers between devices with their start and end apart: 3 -> 2, of which waited for: 2 -> 1; matrix products, arithmetic and copies ran while one was open for 16% -> 18% of each run, Pallas kernels for 39% -> 50%
where the time goes in v3:
time: 129 us
  Pallas kernels  64.3 us (50%)
  between operations  14.3 us (11%)
  other arithmetic  13.6 us (11%)
  waiting for transfers between devices  12 us (9%)
  matrix products  10.5 us (8%)
  local copies, waits for them, and re-layouts  8.11 us (6%)
  blocking collectives  5.99 us (5%)
    pallas_call x1, Pallas kernels, exchange(): pl.pallas_call(functools.partial(kernel, width), out_shape=(jax.ShapeDtyp...  64.3 us
    reduce_scatter x1, waiting for transfers between devices, on_device(): lax.psum_scatter(text_part, 'tp', scatter_dimension=1, tiled=True)  11.3 us
    all_gather x1, blocking collectives, on_device(): meta = lax.all_gather(jnp.stack([offsets, counts]), 'section', axis=0)  5.99 us
    dot_general x4, matrix products, on_device(): jnp.dot(text_gain, w_all[s], preferred_element_type=f32)  5.83 us
    dot_general x2, matrix products, on_device(): jnp.dot(grads[h], w_own_t[h * half:(h + 1) * half], preferred_element_typ...  4.69 us
    unnamed x26, local copies, waits for them, and re-layouts  3.13 us
    dynamic_slice x1, local copies, waits for them, and re-layouts, on_device(): lax.dynamic_slice_in_dim(text_tokens, (f * pairs + pair) * part, part, ax...  2.86 us
  transfers between devices with their start and end apart: 2, of which 1 were waited for; matrix products, arithmetic and copies ran while one was open for 18% of the time, Pallas kernels for 50%

profile of v3, /device:TPU:0, one launch (start us, length us, event | category | flops | bytes accessed | tf_op | source)
XLA Modules:
  0.0 128.9 jit_solution(15831593672163545717)
XLA Ops:
  7.2 0.0 copy-start
  7.2 0.0 all-gather.4.cloned.1.call-start
  7.2 0.7 all-gather.4.cloned.1.call-update
  7.9 0.0 reduce-scatter.2.cloned.1.call-start
  8.0 0.7 add_bitcast_fusion
  8.6 6.0 %all-gather.1 = s32[4,2,4]{2,1,0:T(2,128)S(1)} all-gather(s32[1,2,4]{2,1,0:T(2,128)S(1)} %add_bitcast_fusion), channel_id=2, replica_groups=mesh['section'=4,'fsdp'=4,'tp'=2] {'section'}, dimensions={0}, use_global_device_ids=true | all-gather | bytes 160 | tf_op jit(solution)/shard_map/all_gather | solution.py:322
  14.6 1.8 %copy.19 = bf16[1024,128]{0,1:T(8,128)(2,1)} copy(bf16[1024,128]{1,0:T(8,128)(2,1)} %param.12) | data formatting | bytes 524288 | tf_op args[5]
  16.4 0.7 iota_compare_fusion
  17.2 2.1 %fusion = f32[4,256]{1,0:T(4,128)S(1)} fusion(bf16[4,256,1024]{2,1,0:T(8,128)(2,1)} %param.8), kind=kLoop, calls=%fused_computation.4 | loop fusion | flops 3144704 | bytes 2101248 | tf_op jit(solution)/shard_map/reduce_sum | solution.py:350
  19.2 0.6 copy.28
  19.9 0.2 select_reduce_fusion.3
  20.1 0.1 select_reduce_fusion.b_tab
  20.2 0.0 copy-start.9
  20.2 0.1 constant_dynamic-slice_fusion.5
  20.3 1.0 and_select_fusion
  21.3 0.1 select_reduce_fusion.1
  21.4 0.7 fusion.28
  22.1 0.6 pad_add_fusion.1
  22.7 0.6 fusion.27
  23.2 0.8 fusion.25
  24.0 0.0 copy-done
  24.0 0.7 constant_dynamic-slice_fusion.4.vg_ref
  24.7 2.9 %constant_dynamic-slice_fusion.3 = (bf16[256,1024]{1,0:T(8,128)(2,1)S(1)}, bf16[256,1024]{1,0:T(8,128)(2,1)S(1)}, bf16[256,1024]{1,0:T(8,128)(2,1)}, bf16[256,1024]{1,0:T(8,128)(2,1)}) fusion(bf16[256,8192]{1,0:T(8,128)(2,1)} %param.7, s32[]{:T(128)S(6)} %select_n.111, s32[]{:T(128)S(6)} %select_n.112, s32[]{:T(128)S(6)} %select_n.114, s32[]{:T(128)S(6)} %select_n.113), kind=kLoop, calls=%fused_computation.57 | loop fusion | bytes 4194320 | tf_op jit(solution)/shard_map/dynamic_slice | solution.py:371
  27.5 0.0 copy-done.1
  27.6 0.9 multiply_reduce_fusion
  28.5 0.0 copy-done.9
  28.5 0.0 copy-done.2
  28.5 1.9 %fusion.1.img_ref = bf16[1024,1024]{1,0:T(8,128)(2,1)} fusion(bf16[4,256,1024]{2,1,0:T(8,128)(2,1)S(1)} %copy-done.2, f32[1024]{0:T(1024)S(1)} %get-tuple-element.24), kind=kLoop, calls=%fused_computation.5 | loop fusion | flops 3145728 | bytes 4198400 | tf_op jit(solution)/shard_map/convert_element_type | solution.py:349
  30.4 64.3 %shard_map.86 = (bf16[2,1024,256]{2,1,0:T(8,128)(2,1)}, f32[256,256]{1,0:T(8,128)}, f32[1,1024]{1,0:T(1,128)}, f32[1,1024]{1,0:T(1,128)}, bf16[512,1024]{1,0:T(8,128)(2,1)}) custom-call(s32[2,4]{1,0:T(2,128)} %get-tuple-element.34.a_tab, s32[3,4]{1,0:T(4,128)} %copy-done.9, s32[2,4]{1,0:T(2,128)} %get-tuple-element.35.r_tab, ...), custom_call_target="tpu_custom_call" | custom-call | flops 21474836480 | bytes 33554432 | tf_op jit(solution)/shard_map/pallas_call | solution.py:270
  94.7 0.7 add_rsqrt_fusion
  95.4 0.0 all-gather.4.cloned.1.call-done
  95.4 0.0 copy-start.6
  95.4 0.0 copy-start.7
  95.4 0.0 copy-start.10
  95.4 2.4 %fusion.10 = f32[256,128]{1,0:T(8,128)S(1)} fusion(bf16[16384,128]{1,0:T(8,128)(2,1)} %all-gather.4.cloned.1.call-done, bf16[256,1024]{1,0:T(8,128)(2,1)} %get-tuple-element.20, bf16[256,1024]{1,0:T(8,128)(2,1)} %get-tuple-element.21, bf16[256,1024]{1,0:T(8,128)(2,1)S(1)} %get-tuple-element.19, bf16[256,1024]{1,0:T(8,128)(2,1)S(1)} %get-tuple-element.18, ...), kind=kOutput, calls=%fused_computation.16 | convolution fusion | flops 278921216 | bytes 3293184 | tf_op jit(solution)/shard_map/dot_general | solution.py:384
  97.9 0.7 copy-done.10
  98.5 0.7 fusion.8
  99.3 0.7 fusion.6
  100.0 2.0 %fusion.12 = f32[256,128]{1,0:T(8,128)S(1)} fusion(bf16[16384,128]{1,0:T(8,128)(2,1)S(1)} %copy-done.10, bf16[256,1024]{1,0:T(8,128)(2,1)S(1)} %copy-done.6, bf16[256,1024]{1,0:T(8,128)(2,1)S(1)} %copy-done.7, bf16[256,1024]{1,0:T(8,128)(2,1)} %copy-done.5, bf16[256,1024]{1,0:T(8,128)(2,1)} %copy-done.4, f32[4096]{0:T(1024)S(1)} %pad_maximum_fusion), kind=kOutput, calls=%fused_computation.18 | convolution fusion | flops 278921216 | bytes 3293184 | tf_op jit(solution)/shard_map/dot_general | solution.py:384
  102.0 0.9 maximum_multiply_fusion
  102.9 0.0 reduce-scatter.2.cloned.1.call-update
  102.9 1.3 compare_and_fusion
  104.3 1.8 %fusion.15 = f32[1024,1024]{1,0:T(8,128)S(1)} fusion(bf16[512,1024]{1,0:T(8,128)(2,1)} %get-tuple-element.14, bf16[2,1024,256]{2,1,0:T(8,128)(2,1)S(1)} %copy-done.3), kind=kOutput, calls=%fused_computation.22 | convolution fusion | flops 536870912 | bytes 5242880 | tf_op jit(solution)/shard_map/dot_general | solution.py:392
  106.1 0.0 copy-done.8
  106.1 0.0 copy-done.11
  106.1 2.9 %broadcast_select_fusion = bf16[1024,1024]{1,0:T(8,128)(2,1)} fusion(pred[1024]{0:T(1024)(128)(4,1)S(1)} %lt.82, f32[1024]{0:T(1024)S(1)} %bitcast.60, f32[1024]{0:T(1024)S(1)} %multiply_multiply_fusion, bf16[4,256,1024]{2,1,0:T(8,128)(2,1)S(1)} %copy-done.2, f32[1024]{0:T(1024)S(1)} %get-tuple-element.24, f32[1024,1024]{1,0:T(8,128)S(1)} %fusion.15, ...), kind=kOutput, calls=%fused_computation.11 | convolution fusion | flops 547356672 | bytes 9454592 | tf_op jit(solution)/shard_map/dot_general | solution.py:392
  109.0 11.3 %reduce-scatter.2.cloned.1.call-done = f32[256,256]{1,0:T(8,128)} async-done(((f32[256,512]{1,0:T(8,128)}), f32[256,256]{1,0:T(8,128)}) %reduce-scatter.2.cloned.1.call-update) | async-done | bytes 262160 | tf_op jit(solution)/shard_map/reduce_scatter | solution.py:387
  120.3 1.8 %select_convert_fusion = bf16[256,256]{1,0:T(8,128)(2,1)} fusion(f32[256,256]{1,0:T(8,128)} %get-tuple-element.9, f32[256,256]{1,0:T(8,128)} %reduce-scatter.2.cloned.1.call-done, pred[256]{0:T(512)(128)(4,1)S(1)} %compare_and_fusion), kind=kLoop, calls=%fused_computation.28 | loop fusion | flops 65536 | bytes 655616 | tf_op jit(solution)/shard_map/convert_element_type | solution.py:402
  (21 shorter events, 0.1 us)
Async XLA Ops:
  7.2 16.8 %copy-start = (bf16[256,512]{1,0:T(8,128)(2,1)S(1)}, bf16[256,512]{1,0:T(8,128)(2,1)}, u32[]{:S(2)}) copy-start(bf16[256,512]{1,0:T(8,128)(2,1)} %param.13) | copy-start | bytes 786436
  7.2 88.2 %all-gather.4.cloned.1.call-start = ((), (), s32[]{:S(2)}) async-start(), calls=%async_computation.1 | async-start | bytes 4456448 | tf_op jit(solution)/shard_map/all_gather | solution.py:324
  7.9 112.4 %reduce-scatter.2.cloned.1.call-start = ((), (), s32[]{:S(2)}) async-start(), calls=%async_computation.2 | async-start | bytes 786432 | tf_op jit(solution)/shard_map/reduce_scatter | solution.py:387
  19.8 7.7 %copy-start.1 = (bf16[256,8192]{1,0:T(8,128)(2,1)S(1)}, bf16[256,8192]{1,0:T(8,128)(2,1)}, u32[]{:S(2)}) copy-start(bf16[256,8192]{1,0:T(8,128)(2,1)} %param.7) | copy-start | bytes 12582916
  20.2 8.3 %copy-start.9 = (s32[3,4]{1,0:T(4,128)}, s32[3,4]{1,0:T(4,128)S(1)}, u32[]{:S(2)}) copy-start(s32[3,4]{1,0:T(4,128)S(1)} %select_reduce_fusion.b_tab) | copy-start | bytes 148
  24.7 3.8 %copy-start.2 = (bf16[4,256,1024]{2,1,0:T(8,128)(2,1)S(1)}, bf16[4,256,1024]{2,1,0:T(8,128)(2,1)}, u32[]{:S(2)}) copy-start(bf16[4,256,1024]{2,1,0:T(8,128)(2,1)} %param.8) | copy-start | bytes 6291460
  27.5 71.7 %copy-start.4 = (bf16[256,1024]{1,0:T(8,128)(2,1)}, bf16[256,1024]{1,0:T(8,128)(2,1)S(1)}, u32[]{:S(2)}) copy-start(bf16[256,1024]{1,0:T(8,128)(2,1)S(1)} %get-tuple-element.18) | copy-start | bytes 1572868
  27.5 71.7 %copy-start.5 = (bf16[256,1024]{1,0:T(8,128)(2,1)}, bf16[256,1024]{1,0:T(8,128)(2,1)S(1)}, u32[]{:S(2)}) copy-start(bf16[256,1024]{1,0:T(8,128)(2,1)S(1)} %get-tuple-element.19) | copy-start | bytes 1572868
  95.4 2.4 %copy-start.6 = (bf16[256,1024]{1,0:T(8,128)(2,1)S(1)}, bf16[256,1024]{1,0:T(8,128)(2,1)}, u32[]{:S(2)}) copy-start(bf16[256,1024]{1,0:T(8,128)(2,1)} %get-tuple-element.20) | copy-start | bytes 1572868
  95.4 2.4 %copy-start.7 = (bf16[256,1024]{1,0:T(8,128)(2,1)S(1)}, bf16[256,1024]{1,0:T(8,128)(2,1)}, u32[]{:S(2)}) copy-start(bf16[256,1024]{1,0:T(8,128)(2,1)} %get-tuple-element.21) | copy-start | bytes 1572868
  95.4 3.1 %copy-start.10 = (bf16[16384,128]{1,0:T(8,128)(2,1)S(1)}, bf16[16384,128]{1,0:T(8,128)(2,1)}, u32[]{:S(2)}) copy-start(bf16[16384,128]{1,0:T(8,128)(2,1)} %all-gather.4.cloned.1.call-done) | copy-start | bytes 12582916
  100.0 4.2 %copy-start.3 = (bf16[2,1024,256]{2,1,0:T(8,128)(2,1)S(1)}, bf16[2,1024,256]{2,1,0:T(8,128)(2,1)}, u32[]{:S(2)}) copy-start(bf16[2,1024,256]{2,1,0:T(8,128)(2,1)} %get-tuple-element.13) | copy-start | bytes 3145732
  104.2 1.9 %copy-start.8 = (bf16[512,1024]{1,0:T(8,128)(2,1)S(1)}, bf16[512,1024]{1,0:T(8,128)(2,1)}, u32[]{:S(2)}) copy-start(bf16[512,1024]{1,0:T(8,128)(2,1)} %get-tuple-element.14) | copy-start | bytes 3145732
  104.2 1.9 %copy-start.11 = (f32[1,1024]{1,0:T(1,128)S(1)}, f32[1,1024]{1,0:T(1,128)}, u32[]{:S(2)}) copy-start(f32[1,1024]{1,0:T(1,128)} %get-tuple-element.15) | copy-start | bytes 12292
Sparse Core Ops, SparseCore 0:
  10.2 62.2 all-gather.3
  103.1 17.1 reduce-scatter.1

commit v4 on v3

--- a/solution.py
+++ b/solution.py
@@ -384,7 +384,11 @@
         [jnp.dot(text_gain, w_all[s], preferred_element_type=f32) for s in range(sections)], axis=1
     )
     grads, text_part = lax.optimization_barrier((grads, text_part))
-    text_values = lax.psum_scatter(text_part, "tp", scatter_dimension=1, tiled=True)
+    text_values = lax.dynamic_slice_in_dim(text_part, pair * half, half, axis=1)
+    for d in range(1, pairs):
+        theirs = lax.dynamic_slice_in_dim(text_part, lax.rem(pair + d, pairs) * half, half, axis=1)
+        moved = lax.ppermute(theirs.astype(bf16), "tp", [(p, (p + d) % pairs) for p in range(pairs)])
+        text_values = text_values + moved.astype(f32)
     square_sum = square_sum.reshape(-1, 1)
     inner = inner.reshape(-1, 1)
     inv_rms = lax.rsqrt(square_sum / width + epsilon)

time: 129 us -> 117 us (0.907)
  waiting for transfers between devices: 12 us -> 0.7 us
  matrix products: 10.5 us -> 8.17 us
  starting transfers between devices: 0.08 us -> 2.05 us
  other arithmetic: 13.6 us -> 12 us
    reduce_scatter x1 -> x0, waiting for transfers between devices: 11.3 us -> none  [on_device(): lax.psum_scatter(text_part, 'tp', scatter_dimension=1, tiled=True)]
    ppermute x0 -> x1, starting transfers between devices: none -> 2.01 us  [on_device(): lax.ppermute(theirs.astype(bf16), 'tp', [(p, (p + d) % pairs) for p in ra...]
    dot_general x4, matrix products: 5.83 us -> 4.54 us  [on_device(): jnp.dot(text_gain, w_all[s], preferred_element_type=f32)]
    unnamed x26 -> x24, local copies, waits for them, and re-layouts: 3.13 us -> 3.12 us
  transfers between devices with their start and end apart: 2 -> 2, of which waited for: 1 -> 0; matrix products, arithmetic and copies ran while one was open for 18% -> 19% of each run, Pallas kernels for 50% -> 56%
where the time goes in v4:
time: 117 us; the launch traced here: 116 us
  Pallas kernels  64.4 us (55%)
  between operations  14.2 us (12%)
  other arithmetic  12 us (10%)
  matrix products  8.17 us (7%)
  local copies, waits for them, and re-layouts  8.09 us (7%)
  blocking collectives  5.99 us (5%)
  starting transfers between devices  2.05 us (2%)
    pallas_call x1, Pallas kernels, exchange(): pl.pallas_call(functools.partial(kernel, width), out_shape=(jax.ShapeDtyp...  64.4 us
    all_gather x1, blocking collectives, on_device(): meta = lax.all_gather(jnp.stack([offsets, counts]), 'section', axis=0)  5.99 us
    dot_general x4, matrix products, on_device(): jnp.dot(text_gain, w_all[s], preferred_element_type=f32)  4.54 us
    dot_general x2, matrix products, on_device(): jnp.dot(grads[h], w_own_t[h * half:(h + 1) * half], preferred_element_typ...  3.63 us
    unnamed x24, local copies, waits for them, and re-layouts  3.12 us
    dynamic_slice x1, local copies, waits for them, and re-layouts, on_device(): lax.dynamic_slice_in_dim(text_tokens, (f * pairs + pair) * part, part, ax...  2.89 us
  transfers between devices with their start and end apart: 2, of which 0 were waited for; matrix products, arithmetic and copies ran while one was open for 19% of the time, Pallas kernels for 56%

profile of v4, /device:TPU:0, one launch (start us, length us, event | category | flops | bytes accessed | tf_op | source)
XLA Modules:
  0.0 115.6 jit_solution(9751834354978060297)
XLA Ops:
  7.2 0.0 copy-start
  7.2 0.0 all-gather.4.cloned.1.call-start
  7.2 0.7 all-gather.4.cloned.1.call-update
  7.9 0.7 add_bitcast_fusion
  8.6 6.0 %all-gather.1 = s32[4,2,4]{2,1,0:T(2,128)S(1)} all-gather(s32[1,2,4]{2,1,0:T(2,128)S(1)} %add_bitcast_fusion), channel_id=2, replica_groups=mesh['section'=4,'fsdp'=4,'tp'=2] {'section'}, dimensions={0}, use_global_device_ids=true | all-gather | bytes 160 | tf_op jit(solution)/shard_map/all_gather | solution.py:322
  14.6 1.8 %copy.19 = bf16[1024,128]{0,1:T(8,128)(2,1)} copy(bf16[1024,128]{1,0:T(8,128)(2,1)} %param.12) | data formatting | bytes 524288 | tf_op args[5]
  16.4 0.7 iota_compare_fusion
  17.1 2.1 %fusion = f32[4,256]{1,0:T(4,128)S(1)} fusion(bf16[4,256,1024]{2,1,0:T(8,128)(2,1)} %param.8), kind=kLoop, calls=%fused_computation.4 | loop fusion | flops 3144704 | bytes 2101248 | tf_op jit(solution)/shard_map/reduce_sum | solution.py:350
  19.2 0.6 copy.28
  19.8 0.2 select_reduce_fusion.3
  20.0 0.1 select_reduce_fusion.b_tab
  20.2 0.0 copy-start.8
  20.2 0.1 constant_dynamic-slice_fusion.5
  20.2 0.5 fusion.27
  20.8 1.8 %compare_and_fusion = pred[256]{0:T(512)(128)(4,1)S(1)} fusion(s32[]{:T(128)} %bitcast.8, s32[]{:T(128)} %bitcast.7, s32[]{:T(128)S(6)} %select_n.102), kind=kLoop, calls=%fused_computation.58 | loop fusion | flops 1024 | bytes 268 | tf_op jit(solution)/shard_map/and | solution.py:366
  22.5 0.7 and_select_fusion
  23.2 0.1 select_reduce_fusion.1
  23.3 0.7 fusion.28
  24.0 0.6 pad_add_fusion.1
  24.6 0.8 fusion.25
  25.3 0.0 copy-done
  25.3 0.7 constant_dynamic-slice_fusion.4.vg_ref
  26.0 2.9 %constant_dynamic-slice_fusion.3 = (bf16[256,1024]{1,0:T(8,128)(2,1)S(1)}, bf16[256,1024]{1,0:T(8,128)(2,1)S(1)}, bf16[256,1024]{1,0:T(8,128)(2,1)}, bf16[256,1024]{1,0:T(8,128)(2,1)}) fusion(bf16[256,8192]{1,0:T(8,128)(2,1)} %param.7, s32[]{:T(128)S(6)} %select_n.115, s32[]{:T(128)S(6)} %select_n.116, s32[]{:T(128)S(6)} %select_n.118, s32[]{:T(128)S(6)} %select_n.117), kind=kLoop, calls=%fused_computation.53 | loop fusion | bytes 4194320 | tf_op jit(solution)/shard_map/dynamic_slice | solution.py:371
  28.9 0.0 copy-done.1
  28.9 0.9 multiply_reduce_fusion
  29.8 0.0 copy-done.8
  29.8 0.0 copy-done.2
  29.8 1.9 %fusion.1.img_ref = bf16[1024,1024]{1,0:T(8,128)(2,1)} fusion(bf16[4,256,1024]{2,1,0:T(8,128)(2,1)S(1)} %copy-done.2, f32[1024]{0:T(1024)S(1)} %get-tuple-element.24), kind=kLoop, calls=%fused_computation.5 | loop fusion | flops 3145728 | bytes 4198400 | tf_op jit(solution)/shard_map/convert_element_type | solution.py:349
  31.7 64.4 %shard_map.86 = (bf16[2,1024,256]{2,1,0:T(8,128)(2,1)}, f32[256,256]{1,0:T(8,128)}, f32[1,1024]{1,0:T(1,128)}, f32[1,1024]{1,0:T(1,128)}, bf16[512,1024]{1,0:T(8,128)(2,1)}) custom-call(s32[2,4]{1,0:T(2,128)} %get-tuple-element.34.a_tab, s32[3,4]{1,0:T(4,128)} %copy-done.8, s32[2,4]{1,0:T(2,128)} %get-tuple-element.35.r_tab, ...), custom_call_target="tpu_custom_call" | custom-call | flops 21474836480 | bytes 33554432 | tf_op jit(solution)/shard_map/pallas_call | solution.py:270
  96.2 0.7 add_rsqrt_fusion
  96.9 0.0 all-gather.4.cloned.1.call-done
  96.9 0.0 copy-start.4
  96.9 0.0 copy-start.5
  96.9 0.0 copy-start.9
  96.9 2.4 %fusion.10 = f32[256,128]{1,0:T(8,128)S(1)} fusion(bf16[16384,128]{1,0:T(8,128)(2,1)} %all-gather.4.cloned.1.call-done, bf16[256,1024]{1,0:T(8,128)(2,1)} %get-tuple-element.20, bf16[256,1024]{1,0:T(8,128)(2,1)} %get-tuple-element.21, bf16[256,1024]{1,0:T(8,128)(2,1)S(1)} %get-tuple-element.19, bf16[256,1024]{1,0:T(8,128)(2,1)S(1)} %get-tuple-element.18, ...), kind=kOutput, calls=%fused_computation.16 | convolution fusion | flops 278921216 | bytes 3293184 | tf_op jit(solution)/shard_map/dot_general | solution.py:384
  99.4 0.0 copy-done.4
  99.4 0.7 copy-done.9
  100.1 0.7 fusion.8
  100.8 0.7 fusion.6
  101.5 0.7 fusion.12
  102.2 0.1 maximum_multiply_fusion
  102.4 2.0 %collective-permute-start = (bf16[256,256]{1,0:T(8,128)(2,1)S(1)}, bf16[256,256]{1,0:T(8,128)(2,1)S(1)}, u32[]{:S(2)}, u32[]{:S(2)}) collective-permute-start(bf16[256,256]{1,0:T(8,128)(2,1)S(1)} %dynamic-slice_convert_fusion), channel_id=1, source_target_pairs={{0,1},{1,0},{2,3},{3,2},{4,5},{5,4},{6,7},{7,6},{8,9},{9,8},{10,11... | collective-permute-start | bytes 393224 | tf_op jit(solution)/shard_map/ppermute | solution.py:390
  104.4 0.7 fusion.15
  105.1 0.0 copy-done.10
  105.1 0.0 copy-start.7
  105.1 2.9 %broadcast_select_fusion = bf16[1024,1024]{1,0:T(8,128)(2,1)} fusion(pred[1024]{0:T(1024)(128)(4,1)S(1)} %lt.87, f32[1024]{0:T(1024)S(1)} %bitcast.60, f32[1024]{0:T(1024)S(1)} %multiply_multiply_fusion, bf16[4,256,1024]{2,1,0:T(8,128)(2,1)S(1)} %copy-done.2, f32[1024]{0:T(1024)S(1)} %get-tuple-element.24, f32[1024,1024]{1,0:T(8,128)S(1)} %fusion.15, ...), kind=kOutput, calls=%fused_computation.11 | convolution fusion | flops 547356672 | bytes 9454592 | tf_op jit(solution)/shard_map/dot_general | solution.py:396
  108.0 0.0 collective-permute-done
  108.0 0.8 select_convert_fusion
  (19 shorter events, 0.1 us)
Async XLA Ops:
  7.2 18.2 %copy-start = (bf16[256,512]{1,0:T(8,128)(2,1)S(1)}, bf16[256,512]{1,0:T(8,128)(2,1)}, u32[]{:S(2)}) copy-start(bf16[256,512]{1,0:T(8,128)(2,1)} %param.13) | copy-start | bytes 786436
  7.2 89.7 %all-gather.4.cloned.1.call-start = ((), (), s32[]{:S(2)}) async-start(), calls=%async_computation | async-start | bytes 4456448 | tf_op jit(solution)/shard_map/all_gather | solution.py:324
  19.8 9.1 %copy-start.1 = (bf16[256,8192]{1,0:T(8,128)(2,1)S(1)}, bf16[256,8192]{1,0:T(8,128)(2,1)}, u32[]{:S(2)}) copy-start(bf16[256,8192]{1,0:T(8,128)(2,1)} %param.7) | copy-start | bytes 12582916
  20.2 9.7 %copy-start.8 = (s32[3,4]{1,0:T(4,128)}, s32[3,4]{1,0:T(4,128)S(1)}, u32[]{:S(2)}) copy-start(s32[3,4]{1,0:T(4,128)S(1)} %select_reduce_fusion.b_tab) | copy-start | bytes 148
  26.0 3.8 %copy-start.2 = (bf16[4,256,1024]{2,1,0:T(8,128)(2,1)S(1)}, bf16[4,256,1024]{2,1,0:T(8,128)(2,1)}, u32[]{:S(2)}) copy-start(bf16[4,256,1024]{2,1,0:T(8,128)(2,1)} %param.8) | copy-start | bytes 6291460
  96.9 2.4 %copy-start.4 = (bf16[256,1024]{1,0:T(8,128)(2,1)S(1)}, bf16[256,1024]{1,0:T(8,128)(2,1)}, u32[]{:S(2)}) copy-start(bf16[256,1024]{1,0:T(8,128)(2,1)} %get-tuple-element.20) | copy-start | bytes 1572868
  96.9 2.4 %copy-start.5 = (bf16[256,1024]{1,0:T(8,128)(2,1)S(1)}, bf16[256,1024]{1,0:T(8,128)(2,1)}, u32[]{:S(2)}) copy-start(bf16[256,1024]{1,0:T(8,128)(2,1)} %get-tuple-element.21) | copy-start | bytes 1572868
  96.9 3.1 %copy-start.9 = (bf16[16384,128]{1,0:T(8,128)(2,1)S(1)}, bf16[16384,128]{1,0:T(8,128)(2,1)}, u32[]{:S(2)}) copy-start(bf16[16384,128]{1,0:T(8,128)(2,1)} %all-gather.4.cloned.1.call-done) | copy-start | bytes 12582916
  101.5 2.9 %copy-start.3 = (bf16[2,1024,256]{2,1,0:T(8,128)(2,1)S(1)}, bf16[2,1024,256]{2,1,0:T(8,128)(2,1)}, u32[]{:S(2)}) copy-start(bf16[2,1024,256]{2,1,0:T(8,128)(2,1)} %get-tuple-element.13) | copy-start | bytes 3145732
  101.5 2.9 %copy-start.6 = (bf16[512,1024]{1,0:T(8,128)(2,1)S(1)}, bf16[512,1024]{1,0:T(8,128)(2,1)}, u32[]{:S(2)}) copy-start(bf16[512,1024]{1,0:T(8,128)(2,1)} %get-tuple-element.14) | copy-start | bytes 3145732
  102.4 5.7 %collective-permute-start = (bf16[256,256]{1,0:T(8,128)(2,1)S(1)}, bf16[256,256]{1,0:T(8,128)(2,1)S(1)}, u32[]{:S(2)}, u32[]{:S(2)}) collective-permute-start(bf16[256,256]{1,0:T(8,128)(2,1)S(1)} %dynamic-slice_convert_fusion), channel_id=1, source_target_pairs={{0,1},{1,0},{2,3},{3,2},{4,5},{5,4},{6,7},{7,6},{8,9},{9,8},{10,11... | collective-permute-start | bytes 393224 | tf_op jit(solution)/shard_map/ppermute | solution.py:390
  104.4 0.7 copy-start.10
  105.1 2.9 %copy-start.7 = (f32[256,256]{1,0:T(8,128)S(1)}, f32[256,256]{1,0:T(8,128)}, u32[]{:S(2)}) copy-start(f32[256,256]{1,0:T(8,128)} %get-tuple-element.9) | copy-start | bytes 786436
Sparse Core Ops, SparseCore 0:
  10.2 62.8 all-gather.3

commit v5 on v4

--- a/solution.py
+++ b/solution.py
@@ -130,6 +130,14 @@
             one_hot(n, m, start, lo, hi), ref[...], preferred_element_type=f32
         ).astype(bf16)
 
+    def choose(start, ref):
+        def step(i, acc):
+            return jnp.where(start == i * slots, ref[slot(i, slots)].astype(f32), acc)
+
+        return lax.fori_loop(0, ref.shape[0] // slots, step, jnp.zeros((slots, half), f32)).astype(
+            bf16
+        )
+
     eye = lax.broadcasted_iota(jnp.int32, (128, 128), 0) == lax.broadcasted_iota(
         jnp.int32, (128, 128), 1
     )
@@ -180,7 +188,7 @@
         copy(gout.at[s], gin.at[slot(s, slots)], s_a2.at[s], r_a2.at[s], on_s(s)).wait_recv()
 
     def order(k, carry):
-        ghalf[slot(k, slots)] = pick(slots, r_tab[0, k], 0, slots, gin)
+        ghalf[slot(k, slots)] = choose(r_tab[0, k], gin)
         return carry
 
     lax.fori_loop(0, tiles, order, 0)
@@ -199,7 +207,7 @@
         acc = acc + pin[t].astype(f32)
     psum[...] = acc.astype(bf16)
     for s in others_s + [me_s]:
-        block = pick(slots, r_tab[1, s], 0, slots, psum)
+        block = choose(r_tab[1, s], psum)
         if s is me_s:
             bin_[slot(s, slots)] = block
         else:

time: 117 us -> 117 us (level)
  no operation moved by 1% of the time
where the time goes in v5:
time: 117 us; the launch traced here: 115 us
  Pallas kernels  64.1 us (55%)
  between operations  14.2 us (12%)
  other arithmetic  12 us (10%)
  matrix products  8.18 us (7%)
  local copies, waits for them, and re-layouts  8.09 us (7%)
  blocking collectives  5.99 us (5%)
  starting transfers between devices  2.04 us (2%)
    pallas_call x1, Pallas kernels, exchange(): pl.pallas_call(functools.partial(kernel, width), out_shape=(jax.ShapeDtyp...  64.1 us
    all_gather x1, blocking collectives, on_device(): meta = lax.all_gather(jnp.stack([offsets, counts]), 'section', axis=0)  5.99 us
    dot_general x4, matrix products, on_device(): jnp.dot(text_gain, w_all[s], preferred_element_type=f32)  4.54 us
    dot_general x2, matrix products, on_device(): jnp.dot(grads[h], w_own_t[h * half:(h + 1) * half], preferred_element_typ...  3.64 us
    unnamed x24, local copies, waits for them, and re-layouts  3.12 us
    dynamic_slice x1, local copies, waits for them, and re-layouts, on_device(): lax.dynamic_slice_in_dim(text_tokens, (f * pairs + pair) * part, part, ax...  2.89 us
  transfers between devices with their start and end apart: 2, of which 0 were waited for; matrix products, arithmetic and copies ran while one was open for 19% of the time, Pallas kernels for 56%

profile of v5, /device:TPU:0, one launch (start us, length us, event | category | flops | bytes accessed | tf_op | source)
XLA Modules:
  0.0 115.3 jit_solution(14057473001422586187)
XLA Ops:
  7.2 0.0 copy-start
  7.2 0.0 all-gather.4.cloned.1.call-start
  7.2 0.7 all-gather.4.cloned.1.call-update
  7.9 0.7 add_bitcast_fusion
  8.6 6.0 %all-gather.1 = s32[4,2,4]{2,1,0:T(2,128)S(1)} all-gather(s32[1,2,4]{2,1,0:T(2,128)S(1)} %add_bitcast_fusion), channel_id=2, replica_groups=mesh['section'=4,'fsdp'=4,'tp'=2] {'section'}, dimensions={0}, use_global_device_ids=true | all-gather | bytes 160 | tf_op jit(solution)/shard_map/all_gather | solution.py:330
  14.6 1.8 %copy.19 = bf16[1024,128]{0,1:T(8,128)(2,1)} copy(bf16[1024,128]{1,0:T(8,128)(2,1)} %param.12) | data formatting | bytes 524288 | tf_op args[5]
  16.4 0.7 iota_compare_fusion
  17.1 2.1 %fusion = f32[4,256]{1,0:T(4,128)S(1)} fusion(bf16[4,256,1024]{2,1,0:T(8,128)(2,1)} %param.8), kind=kLoop, calls=%fused_computation.4 | loop fusion | flops 3144704 | bytes 2101248 | tf_op jit(solution)/shard_map/reduce_sum | solution.py:358
  19.2 0.6 copy.28
  19.8 0.2 select_reduce_fusion.3
  20.0 0.1 select_reduce_fusion.b_tab
  20.2 0.0 copy-start.8
  20.2 0.1 constant_dynamic-slice_fusion.5
  20.2 0.5 fusion.27
  20.8 1.8 %compare_and_fusion = pred[256]{0:T(512)(128)(4,1)S(1)} fusion(s32[]{:T(128)} %bitcast.8, s32[]{:T(128)} %bitcast.7, s32[]{:T(128)S(6)} %select_n.102), kind=kLoop, calls=%fused_computation.58 | loop fusion | flops 1024 | bytes 268 | tf_op jit(solution)/shard_map/and | solution.py:374
  22.5 0.7 and_select_fusion
  23.2 0.1 select_reduce_fusion.1
  23.3 0.7 fusion.28
  24.0 0.6 pad_add_fusion.1
  24.6 0.8 fusion.25
  25.3 0.0 copy-done
  25.3 0.7 constant_dynamic-slice_fusion.4.vg_ref
  26.0 2.9 %constant_dynamic-slice_fusion.3 = (bf16[256,1024]{1,0:T(8,128)(2,1)S(1)}, bf16[256,1024]{1,0:T(8,128)(2,1)S(1)}, bf16[256,1024]{1,0:T(8,128)(2,1)}, bf16[256,1024]{1,0:T(8,128)(2,1)}) fusion(bf16[256,8192]{1,0:T(8,128)(2,1)} %param.7, s32[]{:T(128)S(6)} %select_n.115, s32[]{:T(128)S(6)} %select_n.116, s32[]{:T(128)S(6)} %select_n.118, s32[]{:T(128)S(6)} %select_n.117), kind=kLoop, calls=%fused_computation.53 | loop fusion | bytes 4194320 | tf_op jit(solution)/shard_map/dynamic_slice | solution.py:379
  28.9 0.0 copy-done.1
  28.9 0.9 multiply_reduce_fusion
  29.8 0.0 copy-done.8
  29.8 0.0 copy-done.2
  29.8 1.9 %fusion.1.img_ref = bf16[1024,1024]{1,0:T(8,128)(2,1)} fusion(bf16[4,256,1024]{2,1,0:T(8,128)(2,1)S(1)} %copy-done.2, f32[1024]{0:T(1024)S(1)} %get-tuple-element.24), kind=kLoop, calls=%fused_computation.5 | loop fusion | flops 3145728 | bytes 4198400 | tf_op jit(solution)/shard_map/convert_element_type | solution.py:357
  31.7 64.1 %shard_map.86 = (bf16[2,1024,256]{2,1,0:T(8,128)(2,1)}, f32[256,256]{1,0:T(8,128)}, f32[1,1024]{1,0:T(1,128)}, f32[1,1024]{1,0:T(1,128)}, bf16[512,1024]{1,0:T(8,128)(2,1)}) custom-call(s32[2,4]{1,0:T(2,128)} %get-tuple-element.34.a_tab, s32[3,4]{1,0:T(4,128)} %copy-done.8, s32[2,4]{1,0:T(2,128)} %get-tuple-element.35.r_tab, ...), custom_call_target="tpu_custom_call" | custom-call | flops 21474836480 | bytes 33554432 | tf_op jit(solution)/shard_map/pallas_call | solution.py:278
  95.8 0.7 add_rsqrt_fusion
  96.5 0.0 all-gather.4.cloned.1.call-done
  96.5 0.0 copy-start.4
  96.5 0.0 copy-start.5
  96.6 0.0 copy-start.9
  96.6 2.4 %fusion.10 = f32[256,128]{1,0:T(8,128)S(1)} fusion(bf16[16384,128]{1,0:T(8,128)(2,1)} %all-gather.4.cloned.1.call-done, bf16[256,1024]{1,0:T(8,128)(2,1)} %get-tuple-element.20, bf16[256,1024]{1,0:T(8,128)(2,1)} %get-tuple-element.21, bf16[256,1024]{1,0:T(8,128)(2,1)S(1)} %get-tuple-element.19, bf16[256,1024]{1,0:T(8,128)(2,1)S(1)} %get-tuple-element.18, ...), kind=kOutput, calls=%fused_computation.16 | convolution fusion | flops 278921216 | bytes 3293184 | tf_op jit(solution)/shard_map/dot_general | solution.py:392
  99.0 0.0 copy-done.4
  99.0 0.0 copy-done.5
  99.0 0.7 copy-done.9
  99.7 0.7 fusion.8
  100.4 0.7 fusion.6
  101.1 0.7 fusion.12
  101.9 0.1 maximum_multiply_fusion
  102.0 2.0 %collective-permute-start = (bf16[256,256]{1,0:T(8,128)(2,1)S(1)}, bf16[256,256]{1,0:T(8,128)(2,1)S(1)}, u32[]{:S(2)}, u32[]{:S(2)}) collective-permute-start(bf16[256,256]{1,0:T(8,128)(2,1)S(1)} %dynamic-slice_convert_fusion), channel_id=1, source_target_pairs={{0,1},{1,0},{2,3},{3,2},{4,5},{5,4},{6,7},{7,6},{8,9},{9,8},{10,11... | collective-permute-start | bytes 393224 | tf_op jit(solution)/shard_map/ppermute | solution.py:398
  104.0 0.0 copy-done.3
  104.0 0.7 fusion.15
  104.7 2.9 %broadcast_select_fusion = bf16[1024,1024]{1,0:T(8,128)(2,1)} fusion(pred[1024]{0:T(1024)(128)(4,1)S(1)} %lt.87, f32[1024]{0:T(1024)S(1)} %bitcast.60, f32[1024]{0:T(1024)S(1)} %multiply_multiply_fusion, bf16[4,256,1024]{2,1,0:T(8,128)(2,1)S(1)} %copy-done.2, f32[1024]{0:T(1024)S(1)} %get-tuple-element.24, f32[1024,1024]{1,0:T(8,128)S(1)} %fusion.15, ...), kind=kOutput, calls=%fused_computation.11 | convolution fusion | flops 547356672 | bytes 9454592 | tf_op jit(solution)/shard_map/dot_general | solution.py:404
  107.7 0.0 collective-permute-done
  107.7 0.8 select_convert_fusion
  (19 shorter events, 0.1 us)
Async XLA Ops:
  7.2 18.2 %copy-start = (bf16[256,512]{1,0:T(8,128)(2,1)S(1)}, bf16[256,512]{1,0:T(8,128)(2,1)}, u32[]{:S(2)}) copy-start(bf16[256,512]{1,0:T(8,128)(2,1)} %param.13) | copy-start | bytes 786436
  7.2 89.3 %all-gather.4.cloned.1.call-start = ((), (), s32[]{:S(2)}) async-start(), calls=%async_computation | async-start | bytes 4456448 | tf_op jit(solution)/shard_map/all_gather | solution.py:332
  19.8 9.1 %copy-start.1 = (bf16[256,8192]{1,0:T(8,128)(2,1)S(1)}, bf16[256,8192]{1,0:T(8,128)(2,1)}, u32[]{:S(2)}) copy-start(bf16[256,8192]{1,0:T(8,128)(2,1)} %param.7) | copy-start | bytes 12582916
  20.2 9.7 %copy-start.8 = (s32[3,4]{1,0:T(4,128)}, s32[3,4]{1,0:T(4,128)S(1)}, u32[]{:S(2)}) copy-start(s32[3,4]{1,0:T(4,128)S(1)} %select_reduce_fusion.b_tab) | copy-start | bytes 148
  26.0 3.8 %copy-start.2 = (bf16[4,256,1024]{2,1,0:T(8,128)(2,1)S(1)}, bf16[4,256,1024]{2,1,0:T(8,128)(2,1)}, u32[]{:S(2)}) copy-start(bf16[4,256,1024]{2,1,0:T(8,128)(2,1)} %param.8) | copy-start | bytes 6291460
  96.5 2.4 %copy-start.4 = (bf16[256,1024]{1,0:T(8,128)(2,1)S(1)}, bf16[256,1024]{1,0:T(8,128)(2,1)}, u32[]{:S(2)}) copy-start(bf16[256,1024]{1,0:T(8,128)(2,1)} %get-tuple-element.20) | copy-start | bytes 1572868
  96.5 2.4 %copy-start.5 = (bf16[256,1024]{1,0:T(8,128)(2,1)S(1)}, bf16[256,1024]{1,0:T(8,128)(2,1)}, u32[]{:S(2)}) copy-start(bf16[256,1024]{1,0:T(8,128)(2,1)} %get-tuple-element.21) | copy-start | bytes 1572868
  96.6 3.1 %copy-start.9 = (bf16[16384,128]{1,0:T(8,128)(2,1)S(1)}, bf16[16384,128]{1,0:T(8,128)(2,1)}, u32[]{:S(2)}) copy-start(bf16[16384,128]{1,0:T(8,128)(2,1)} %all-gather.4.cloned.1.call-done) | copy-start | bytes 12582916
  101.1 2.9 %copy-start.3 = (bf16[2,1024,256]{2,1,0:T(8,128)(2,1)S(1)}, bf16[2,1024,256]{2,1,0:T(8,128)(2,1)}, u32[]{:S(2)}) copy-start(bf16[2,1024,256]{2,1,0:T(8,128)(2,1)} %get-tuple-element.13) | copy-start | bytes 3145732
  101.1 2.9 %copy-start.6 = (bf16[512,1024]{1,0:T(8,128)(2,1)S(1)}, bf16[512,1024]{1,0:T(8,128)(2,1)}, u32[]{:S(2)}) copy-start(bf16[512,1024]{1,0:T(8,128)(2,1)} %get-tuple-element.14) | copy-start | bytes 3145732
  102.0 5.7 %collective-permute-start = (bf16[256,256]{1,0:T(8,128)(2,1)S(1)}, bf16[256,256]{1,0:T(8,128)(2,1)S(1)}, u32[]{:S(2)}, u32[]{:S(2)}) collective-permute-start(bf16[256,256]{1,0:T(8,128)(2,1)S(1)} %dynamic-slice_convert_fusion), channel_id=1, source_target_pairs={{0,1},{1,0},{2,3},{3,2},{4,5},{5,4},{6,7},{7,6},{8,9},{9,8},{10,11... | collective-permute-start | bytes 393224 | tf_op jit(solution)/shard_map/ppermute | solution.py:398
  104.0 0.7 copy-start.10
  104.7 2.9 %copy-start.7 = (f32[256,256]{1,0:T(8,128)S(1)}, f32[256,256]{1,0:T(8,128)}, u32[]{:S(2)}) copy-start(f32[256,256]{1,0:T(8,128)} %get-tuple-element.9) | copy-start | bytes 786436
Sparse Core Ops, SparseCore 0:
  10.2 62.8 all-gather.3
